TPU v7x, 32 devices: a whole 2x2x4 slice. The times are simulated.
32 devices in a mesh: row: 2 (over core), col: 4 (over y, x), seed: 4 (over z).
Axes of the slice: x: 2, y: 2, z: 4, core: 2. Of those that a mesh axis runs over, the one named last changes fastest.
Arguments:
- tiles: bfloat16 [2, 4, 384, 128, 128], P('row', 'col'), may hold values from -0.0390625 to 0.0390625
- tile_out: int32 [2, 4, 384], P('row', 'col'), may hold values from 0 to 1, as said below
- tile_in: int32 [2, 4, 384], P('row', 'col'), may hold values from 0 to 3
- tile_count: int32 [2, 4], P('row', 'col'), may hold values from 1 to 384, as said below
- out_degree: int32 [1024], P(('row', 'col')), may hold values from 1 to 8
- seed_ids: int32 [512, 16], P('seed'), may hold values from 0 to 1023
- prior: float32 [512, 1024], P('seed', ('row', 'col')), may hold values from -6 to 6
Outputs:
- risk: float32 [512, 1024], P('seed', ('row', 'col'))
Inputs may be any that keep to these rules, and one draw needn't show every extreme that they name: `tile_count`: occupied slots of a device come first; some device has all 384 occupied in every draw. `tile_out`: on every device the output blocks named by the occupied slots never fall from one slot to the next; several occupied slots of one device may name the same output block, and the same pair of blocks.
All inputs are finite; a program needn't handle non-finite values.
Results may differ from a plain program's by a relative error of at most 0.0041.
Values may be sent and summed in bfloat16 or wider, within the bound.
No kernel may reach another device: no remote copies, remote signals or barrier semaphores. Data moves between devices by JAX's collectives and lax.ppermute only.
A program may use at most 64 MiB of HBM per device.

v0:
```python
import functools
import math

import jax
import jax.numpy as jnp
from jax import lax
from jax.experimental import pallas as pl
from jax.experimental.pallas import tpu as pltpu
from jax.sharding import PartitionSpec as P

ITERATIONS = 2


damping = 0.85

VMEM = pl.BlockSpec(memory_space=pltpu.VMEM)
SMEM = pl.BlockSpec(memory_space=pltpu.SMEM)
HBM = pl.BlockSpec(memory_space=pltpu.HBM)
ANY = pl.BlockSpec(memory_space=pl.ANY)

TILES_VMEM = 32 * 1024 * 1024
SMALL_VMEM = 8 * 1024 * 1024
LANES = 4
UNROLL = 8
DEGREE_LINES = 8


def in_hbm(*arrays):
    return [pltpu.with_memory_space_constraint(array, pltpu.HBM) for array in arrays]


def call(kernel, out_shape, name, **options):
    return pl.pallas_call(
        kernel,
        out_shape=out_shape,
        compiler_params=pltpu.CompilerParams(vmem_limit_bytes=options.pop("vmem", SMALL_VMEM)),
        cost_estimate=pl.CostEstimate(
            flops=options.pop("flops", 0), bytes_accessed=options.pop("size", 0), transcendentals=0
        ),
        name=name,
        **options,
    )


def partner(index, offset, extent):
    if extent & (extent - 1) == 0:
        return index ^ offset
    return (index + offset) % extent


def from_column(value, cols, offset):
    return lax.ppermute(value, "col", [(partner(col, offset, cols), col) for col in range(cols)])


def hop(row):
    return row + 2


def from_hop(value, cols):
    pairs = [(row * cols + (col ^ hop(row)), row * cols + col) for row in range(2) for col in range(cols)]
    return lax.ppermute(value, ("row", "col"), pairs)


def swap_rows(value):
    return lax.ppermute(value, "row", [(0, 1), (1, 0)])


def scale_kernel(
    prior_hbm, degree_hbm, out_hbm, in_hbm, seeds_hbm,
    scaled_ref, out_ref, in_ref, seeds_ref, prior_ref, degree_ref, arrived,
):
    moves = (
        (prior_hbm, prior_ref), (degree_hbm, degree_ref),
        (out_hbm, out_ref), (in_hbm, in_ref), (seeds_hbm, seeds_ref),
    )
    copies = [
        pltpu.make_async_copy(source, place, arrived.at[index])
        for index, (source, place) in enumerate(moves)
    ]
    for copy in copies:
        copy.start()
    for copy in copies[:2]:
        copy.wait()
    scaled = (prior_ref[...] / degree_ref[...].astype(jnp.float32)).astype(jnp.bfloat16)
    scaled_ref[...] = scaled
    for copy in copies[2:]:
        copy.wait()


def sum_kernel(
    rows, cols, owned_blocks, after_ref, count_ref, out_ref, in_ref, tiles_ref, *rest
):
    *weight_refs, total = rest
    in_blocks = cols * owned_blocks
    slots, edge = tiles_ref.shape[2], tiles_ref.shape[3]
    owned = owned_blocks * edge
    spare = total.shape[1] - 1
    unroll = math.gcd(slots, UNROLL)
    row = lax.axis_index("row")
    occupied = count_ref[0, 0]

    total[...] = jnp.zeros(total.shape, jnp.float32)

    def add_tiles(step, carry):
        at = step * unroll
        places = []
        for lane in range(unroll):
            slot = at + lane
            pair = out_ref[0, 0, slot] * in_blocks + in_ref[0, 0, slot]
            places.append((lane % LANES, jnp.where(slot < occupied, pair, spare), slot))
        for start in range(0, unroll, 2):
            sums = [
                (lane, pair, total[lane, pair] + tiles_ref[0, 0, slot].astype(jnp.float32))
                for lane, pair, slot in places[start:start + 2]
            ]
            for lane, pair, value in sums:
                total[lane, pair] = value
        return carry

    lax.fori_loop(0, (occupied + unroll - 1) // unroll, add_tiles, 0)

    for place in range(rows):
        owner = partner(row, place, rows) if rows == 2 else place
        for block in range(owned_blocks):
            columns = slice(block * edge, (block + 1) * edge)
            for source in range(in_blocks):
                pair = (owner * owned_blocks + block) * in_blocks + source
                value = (total[0, pair] + total[1, pair]) + (total[2, pair] + total[3, pair])
                high = value.astype(jnp.bfloat16)
                low = (value - high.astype(jnp.float32)).astype(jnp.bfloat16)
                column, line = source // owned_blocks, source % owned_blocks * edge
                lines = slice(line, line + edge)
                weight_refs[place][column, lines, columns] = high
                weight_refs[place][column, lines, owned + block * edge:owned + (block + 1) * edge] = low


def times_weight(parts, weights):
    incoming = None
    for start in range(0, len(parts), 2):
        term = jnp.dot(
            jnp.concatenate(parts[start:start + 2], axis=1),
            jnp.concatenate(weights[start:start + 2], axis=0),
            preferred_element_type=jnp.float32,
        )
        incoming = term if incoming is None else incoming + term
    owned = incoming.shape[1] // 2
    return incoming[:, :owned] + incoming[:, owned:]


def product_kernel(rows, cols, after, *refs):
    part_refs, refs = refs[after:after + cols], refs[after + cols:]
    weight_refs, result_refs = refs[:len(refs) // 2], refs[len(refs) // 2:]
    col = lax.axis_index("col")
    parts = [ref[...] for ref in part_refs]
    for weight_ref, result_ref in zip(weight_refs, result_refs):
        weights = [weight_ref[partner(col, offset, cols)] for offset in range(cols)]
        result_ref[...] = times_weight(parts, weights)


def restart_kernel(rows, cols, after_ref, seeds_ref, restart_ref):
    seed_total, sets = seeds_ref.shape
    places, _, owned = restart_ref.shape
    for place in range(places):
        row = partner(lax.axis_index("row"), place, rows)
        first = (row * cols + lax.axis_index("col")) * owned
        vertex = lax.broadcasted_iota(jnp.int32, (owned, sets), 0) + first
        restart = jnp.zeros((owned, sets), jnp.float32)
        for seed in range(seed_total):
            restart += (seeds_ref[seed:seed + 1, :] == vertex).astype(jnp.float32)
        restart_ref[place] = (1.0 - damping) * restart.T


def first_kernel(cols, *refs):
    part_refs, (own_ref, other_ref, degree_ref, given_ref) = refs[:cols], refs[cols:]
    row, col = lax.axis_index("row"), lax.axis_index("col")
    parts = [ref[...] for ref in part_refs]
    sets, owned = parts[0].shape
    columns = [partner(col, offset, cols) for offset in range(cols)]
    wanted = col ^ hop(1 - row)
    for place, weight_ref in enumerate((own_ref, other_ref)):
        given_ref[place, :sets] = times_weight(parts, [weight_ref[column] for column in columns])
        given_ref[place, sets:sets + owned] = weight_ref[wanted, :, :owned].astype(
            jnp.float32
        ) + weight_ref[wanted, :, owned:].astype(jnp.float32)
        given_ref[place, sets + owned:] = jnp.broadcast_to(
            degree_ref[...].astype(jnp.float32), (given_ref.shape[1] - sets - owned, owned)
        )


def both_kernel(mine_ref, theirs_ref, restart_ref, own_ref, scaled_ref):
    _, sets, owned = restart_ref.shape
    for place in range(2):
        incoming = mine_ref[place, :sets] + theirs_ref[1 - place, :sets]
        degree = (theirs_ref if place else mine_ref)[0, sets + owned:sets + owned + 1]
        risk = restart_ref[place] + damping * incoming
        scaled = (risk / degree).astype(jnp.bfloat16)
        scaled_ref[place] = scaled
        if not place:
            own_ref[...] = scaled


def foreign_kernel(after_ref, theirs_ref, weight_ref):
    _, owned, double = weight_ref.shape
    sets = theirs_ref.shape[1] - owned - DEGREE_LINES
    for place in range(2):
        value = theirs_ref[1 - place, sets:sets + owned]
        high = value.astype(jnp.bfloat16)
        weight_ref[place, :, :owned] = high
        weight_ref[place, :, owned:] = (value - high.astype(jnp.float32)).astype(jnp.bfloat16)


def second_kernel(place, after, *refs):
    own_ref, side_ref, hop_ref, weight_ref, foreign_ref, result_ref = refs[after:]
    row, col = lax.axis_index("row"), lax.axis_index("col")
    parts = [own_ref[...], side_ref[...], hop_ref[0], hop_ref[1]]
    weights = [weight_ref[col], weight_ref[col ^ 1], weight_ref[col ^ hop(row)], foreign_ref[place]]
    result_ref[...] = times_weight(parts, weights)


def finish_kernel(last, *refs):
    *incoming_refs, restart_ref, degree_ref, result_ref = refs
    risk = restart_ref[0] + damping * sum(ref[...] for ref in incoming_refs)
    if last:
        result_ref[...] = risk
    else:
        result_ref[...] = (risk / degree_ref[...].astype(jnp.float32)).astype(jnp.bfloat16)


def local(tiles, tile_out, tile_in, tile_count, out_degree, seed_ids, prior):
    rows, cols = lax.axis_size("row"), lax.axis_size("col")
    sets, owned = prior.shape
    slots, edge = tiles.shape[2], tiles.shape[3]
    owned_blocks = owned // edge
    in_blocks, out_blocks = cols * owned_blocks, rows * owned_blocks
    degree = out_degree.reshape(1, owned)
    low = jnp.bfloat16

    scaled, out_ids, in_ids, seeds = call(
        scale_kernel,
        [
            jax.ShapeDtypeStruct((sets, owned), low),
            pltpu.SMEM(tile_out.shape, jnp.int32),
            pltpu.SMEM(tile_in.shape, jnp.int32),
            jax.ShapeDtypeStruct((seed_ids.shape[1], sets), jnp.int32),
        ],
        "scale",
        in_specs=[HBM] * 5,
        out_specs=[VMEM, SMEM, SMEM, VMEM],
        scratch_shapes=[
            pltpu.VMEM((sets, owned), jnp.float32),
            pltpu.VMEM((1, owned), jnp.int32),
            pltpu.SemaphoreType.DMA((5,)),
        ],
        flops=16 * slots * edge**3,
        size=6 * sets * owned,
    )(*in_hbm(prior, degree, tile_out, tile_in, seed_ids.T))

    def spread(value):
        return [from_column(value, cols, offset) if offset else value for offset in range(cols)]

    parts = spread(scaled)

    weights = call(
        functools.partial(sum_kernel, rows, cols, owned_blocks),
        [jax.ShapeDtypeStruct((cols, owned, 2 * owned), low)] * rows,
        "sum_tiles",
        in_specs=[ANY] + [SMEM] * 3 + [VMEM],
        out_specs=[VMEM] * rows,
        scratch_shapes=[pltpu.VMEM((LANES, out_blocks * in_blocks + 1, edge, edge), jnp.float32)],
        vmem=TILES_VMEM,
        flops=slots * edge * edge,
        size=2 * slots * edge * edge,
    )(scaled, tile_count, out_ids, in_ids, tiles)

    piece = jax.ShapeDtypeStruct((sets, owned), jnp.float32)

    def multiply(parts, weights, after=()):
        return call(
            functools.partial(product_kernel, rows, cols, len(after)),
            [piece] * len(weights),
            "product",
            in_specs=[ANY] * len(after) + [VMEM] * (cols + len(weights)),
            out_specs=[VMEM] * len(weights),
            flops=4 * sets * len(weights) * cols * owned * owned,
            size=4 * len(weights) * cols * owned * owned,
        )(*after, *parts, *weights)

    def count_restart(places, after):
        return call(
            functools.partial(restart_kernel, rows, cols),
            jax.ShapeDtypeStruct((places, sets, owned), jnp.float32),
            "restart",
            in_specs=[ANY, VMEM],
            out_specs=VMEM,
            flops=2 * places * sets * owned * seed_ids.shape[1],
            size=4 * places * sets * owned,
        )(after, seeds)

    def finish(incoming, restart, last):
        return call(
            functools.partial(finish_kernel, last),
            piece if last else jax.ShapeDtypeStruct((sets, owned), low),
            "last" if last else "next",
            in_specs=[VMEM] * (len(incoming) + 2),
            out_specs=VMEM,
            size=12 * sets * owned,
        )(*incoming, restart, degree)

    if (rows, cols, ITERATIONS) == (2, 4, 2):
        mine = call(
            functools.partial(first_kernel, cols),
            jax.ShapeDtypeStruct((2, sets + owned + DEGREE_LINES, owned), jnp.float32),
            "first",
            in_specs=[VMEM] * (cols + 3),
            out_specs=VMEM,
            flops=8 * sets * cols * owned * owned,
            size=8 * cols * owned * owned,
        )(*parts, *weights, degree)
        theirs = swap_rows(mine)
        restart = count_restart(2, mine)
        own, both = call(
            both_kernel,
            [jax.ShapeDtypeStruct((sets, owned), low), jax.ShapeDtypeStruct((2, sets, owned), low)],
            "both",
            in_specs=[VMEM] * 3,
            out_specs=[VMEM] * 2,
            size=24 * sets * owned,
        )(mine, theirs, restart)
        side = from_column(own, cols, 1)
        near = from_hop(both, cols)
        foreign = call(
            foreign_kernel,
            jax.ShapeDtypeStruct((2, owned, 2 * owned), low),
            "foreign",
            in_specs=[ANY, VMEM],
            out_specs=VMEM,
            size=16 * owned * owned,
        )(own, theirs)

        def second(place, *after):
            return call(
                functools.partial(second_kernel, place, len(after)),
                piece,
                "second",
                in_specs=[ANY] * len(after) + [VMEM] * 5,
                out_specs=VMEM,
                flops=4 * sets * cols * owned * owned,
                size=4 * cols * owned * owned,
            )(*after, own, side, near, weights[place], foreign)

        leaving = second(1)
        received = swap_rows(leaving)
        return finish((second(0, leaving), received), restart, True)

    for round_index in range(ITERATIONS):
        last = round_index == ITERATIONS - 1
        if rows == 2:
            leaving, = multiply(parts, weights[1:])
            received = swap_rows(leaving)
            staying, = multiply(parts, weights[:1], (leaving,))
            incoming = (staying, received)
        else:
            leaving = jnp.stack(multiply(parts, weights))
            incoming = (lax.psum_scatter(leaving, "row", scatter_dimension=0, tiled=False),)
        if not round_index:
            restart = count_restart(1, leaving)
        value = finish(incoming, restart, last)
        if not last:
            parts = spread(value)
    return value


def solution(mesh):
    placed = (
        P("row", "col", None, None, None),
        P("row", "col", None),
        P("row", "col", None),
        P("row", "col"),
        P(("row", "col")),
        P("seed", None),
        P("seed", ("row", "col")),
    )
    return jax.shard_map(
        local, mesh=mesh, in_specs=placed, out_specs=P("seed", ("row", "col")), check_vma=False
    )
```

profile of v0, /device:TPU:0, one launch (start us, length us, event | category | flops | bytes accessed | tf_op | source)
XLA Modules:
  0.0 20.0 jit_solution(8318220305821665467)
XLA Ops:
  0.0 0.0 copy-start
  0.0 1.1 %scale.1 = (bf16[128,128]{1,0:T(8,128)(2,1)S(1)}, s32[1,1,384]{2,1,0:T(1,128)S(4)}, s32[1,1,384]{2,1,0:T(1,128)S(4)}, s32[16,128]{1,0:T(8,128)S(1)}) custom-call(f32[128,128]{1,0:T(8,128)} %prior_hbm.1, s32[1,128]{1,0:T(1,128)} %bitcast.2, s32[1,1,384]{2,1,0:T(1,128)} %out_hbm.1, s32[1,1,384]{2,1,0:T(1,128)} %in_hbm.1, s32[16,128]{1,0:T(8,128)} %bitcast.5), custom_call_target="tpu_custom_call" | custom-call | flops 12884901888 | bytes 98304 | tf_op jit(solution)/shard_map/scale/pallas_call | solution.py:238
  1.1 0.0 copy-start.1
  1.1 4.0 %collective-permute-start.2 = (bf16[128,128]{1,0:T(8,128)(2,1)S(1)}, bf16[128,128]{1,0:T(8,128)(2,1)S(1)}, u32[]{:S(2)}, u32[]{:S(2)}) collective-permute-start(bf16[128,128]{1,0:T(8,128)(2,1)S(1)} %get-tuple-element.13.after_ref.refs_0_), channel_id=1, source_target_pairs={{12,0},{8,4},{4,8},{0,12},{13,1},{9,5},{5,9},{1,13},{14,2},{10,6},... | collective-permute-start | bytes 98312 | tf_op jit(solution)/shard_map/ppermute | solution.py:52
  5.0 0.5 %collective-permute-start.1 = (bf16[128,128]{1,0:T(8,128)(2,1)S(1)}, bf16[128,128]{1,0:T(8,128)(2,1)S(1)}, u32[]{:S(2)}, u32[]{:S(2)}) collective-permute-start(bf16[128,128]{1,0:T(8,128)(2,1)S(1)} %get-tuple-element.13.after_ref.refs_0_), channel_id=1, source_target_pairs={{8,0},{12,4},{0,8},{4,12},{9,1},{13,5},{1,9},{5,13},{10,2},{14,6},... | collective-permute-start | bytes 98312 | tf_op jit(solution)/shard_map/ppermute | solution.py:52
  5.6 0.1 collective-permute-start
  6.3 0.0 copy-done
  6.4 3.6 %sum_tiles.1 = (bf16[4,128,256]{2,1,0:T(8,128)(2,1)S(1)}, bf16[4,128,256]{2,1,0:T(8,128)(2,1)S(1)}) custom-call(bf16[128,128]{1,0:T(8,128)(2,1)S(1)} %get-tuple-element.13.after_ref.refs_0_, s32[1,1]{1,0:T(1,128)S(6)} %copy.8.count_ref, s32[1,1,384]{2,1,0:T(1,128)S(4)} %get-tuple-element.14.out_ref, s32[1,1,384]{2,1,0:T(1,128)S(4)} %get-tuple-element.15.in_ref, ...), custom_call_target="tpu_custom_call" | custom-call | flops 6291456 | bytes 12582912 | tf_op jit(solution)/shard_map/sum_tiles/pallas_call | solution.py:263
  9.9 0.0 collective-permute-done.2.refs_3_
  9.9 0.0 collective-permute-done.1.refs_2_
  10.0 0.0 collective-permute-done.refs_1_
  10.0 0.0 copy-done.1
  10.0 0.3 %first.1.after_ref.mine_ref = f32[2,264,128]{2,1,0:T(8,128)S(1)} custom-call(bf16[128,128]{1,0:T(8,128)(2,1)S(1)} %get-tuple-element.13.after_ref.refs_0_, bf16[128,128]{1,0:T(8,128)(2,1)S(1)} %collective-permute-done.refs_1_, bf16[128,128]{1,0:T(8,128)(2,1)S(1)} %collective-permute-done.1.refs_2_, bf16[128,128]{1,0:T(8,128)(2,1)S(1)} %collective-permute-done.2.refs_3_, ...), custom_call_target="tpu_custom_call" | custom-call | flops 67108864 | bytes 524288 | tf_op jit(solution)/shard_map/first/pallas_call | solution.py:310
  10.2 0.1 collective-permute-start.3
  10.3 0.3 %restart.1.restart_ref.refs_2_ = f32[2,128,128]{2,1,0:T(8,128)S(1)} custom-call(f32[2,264,128]{2,1,0:T(8,128)S(1)} %first.1.after_ref.mine_ref, s32[16,128]{1,0:T(8,128)S(1)} %get-tuple-element.18.seeds_ref), custom_call_target="tpu_custom_call" | custom-call | flops 1048576 | bytes 131072 | tf_op jit(solution)/shard_map/restart/pallas_call | solution.py:289
  10.6 1.2 %collective-permute-done.3.theirs_ref = f32[2,264,128]{2,1,0:T(8,128)S(1)} collective-permute-done((f32[2,264,128]{2,1,0:T(8,128)S(1)}, f32[2,264,128]{2,1,0:T(8,128)S(1)}, u32[]{:S(2)}, u32[]{:S(2)}) %collective-permute-start.3) | collective-permute-done | bytes 270368 | tf_op jit(solution)/shard_map/ppermute | solution.py:65
  11.9 2.0 %collective-permute-start.5 = (bf16[2,128,128]{2,1,0:T(8,128)(2,1)S(1)}, bf16[2,128,128]{2,1,0:T(8,128)(2,1)S(1)}, u32[]{:S(2)}, u32[]{:S(2)}) collective-permute-start(bf16[2,128,128]{2,1,0:T(8,128)(2,1)S(1)} %get-tuple-element.20), channel_id=1, source_target_pairs={{8,0},{12,4},{0,8},{4,12},{28,16},{24,20},{20,24},{16,28},{9,1},{1... | collective-permute-start | bytes 196616 | tf_op jit(solution)/shard_map/ppermute | solution.py:61
  13.9 1.3 %collective-permute-start.4 = (bf16[128,128]{1,0:T(8,128)(2,1)S(1)}, bf16[128,128]{1,0:T(8,128)(2,1)S(1)}, u32[]{:S(2)}, u32[]{:S(2)}) collective-permute-start(bf16[128,128]{1,0:T(8,128)(2,1)S(1)} %get-tuple-element.19.after_ref.refs_0_.refs_1_), channel_id=1, source_target_pairs={{4,0},{0,4},{12,8},{8,12},{5,1},{1,5},{13,9},{9,13},{6,2},{2,6},{1... | collective-permute-start | bytes 98312 | tf_op jit(solution)/shard_map/ppermute | solution.py:52
  15.2 2.6 %collective-permute-done.4.refs_1_.refs_2_ = bf16[128,128]{1,0:T(8,128)(2,1)S(1)} collective-permute-done((bf16[128,128]{1,0:T(8,128)(2,1)S(1)}, bf16[128,128]{1,0:T(8,128)(2,1)S(1)}, u32[]{:S(2)}, u32[]{:S(2)}) %collective-permute-start.4) | collective-permute-done | bytes 32800 | tf_op jit(solution)/shard_map/ppermute | solution.py:52
  17.8 0.0 collective-permute-done.5.refs_2_.refs_3_
  17.8 0.2 second.2.refs_0_
  18.0 0.1 collective-permute-start.6
  18.1 0.2 %second.3.refs_0_ = f32[128,128]{1,0:T(8,128)S(1)} custom-call(f32[128,128]{1,0:T(8,128)S(1)} %second.2.refs_0_, bf16[128,128]{1,0:T(8,128)(2,1)S(1)} %get-tuple-element.19.after_ref.refs_0_.refs_1_, bf16[128,128]{1,0:T(8,128)(2,1)S(1)} %collective-permute-done.4.refs_1_.refs_2_, bf16[2,128,128]{2,1,0:T(8,128)(2,1)S(1)} %collective-permute-done.5.refs_2_.refs_3_, ...), custom_call_target="tpu_custom_call" | custom-call | flops 33554432 | bytes 262144 | tf_op jit(solution)/shard_map/second/pallas_call | solution.py:341
  18.3 1.0 %collective-permute-done.6.refs_1_ = f32[128,128]{1,0:T(8,128)S(1)} collective-permute-done((f32[128,128]{1,0:T(8,128)S(1)}, f32[128,128]{1,0:T(8,128)S(1)}, u32[]{:S(2)}, u32[]{:S(2)}) %collective-permute-start.6) | collective-permute-done | bytes 65568 | tf_op jit(solution)/shard_map/ppermute | solution.py:65
  19.3 0.7 %last.1 = f32[128,128]{1,0:T(8,128)} custom-call(f32[128,128]{1,0:T(8,128)S(1)} %second.3.refs_0_, f32[128,128]{1,0:T(8,128)S(1)} %collective-permute-done.6.refs_1_, f32[2,128,128]{2,1,0:T(8,128)S(1)} %restart.1.restart_ref.refs_2_, s32[1,128]{1,0:T(1,128)S(1)} %bitcast.4), custom_call_target="tpu_custom_call" | custom-call | bytes 196608 | tf_op jit(solution)/shard_map/last/pallas_call | solution.py:300
  (2 shorter events, 0.1 us)
Async XLA Ops:
  0.0 6.3 %copy-start = (bf16[1,1,384,128,128]{4,3,2,1,0:T(8,128)(2,1)S(1)}, bf16[1,1,384,128,128]{4,3,2,1,0:T(8,128)(2,1)}, u32[]{:S(2)}) copy-start(bf16[1,1,384,128,128]{4,3,2,1,0:T(8,128)(2,1)} %tiles_ref.1) | copy-start | bytes 37748740
  1.1 8.9 %copy-start.1 = (s32[128]{0:T(128)S(1)}, s32[128]{0:T(128)}, u32[]{:S(2)}) copy-start(s32[128]{0:T(128)} %param.11) | copy-start | bytes 1540
  1.1 8.9 %collective-permute-start.2 = (bf16[128,128]{1,0:T(8,128)(2,1)S(1)}, bf16[128,128]{1,0:T(8,128)(2,1)S(1)}, u32[]{:S(2)}, u32[]{:S(2)}) collective-permute-start(bf16[128,128]{1,0:T(8,128)(2,1)S(1)} %get-tuple-element.13.after_ref.refs_0_), channel_id=1, source_target_pairs={{12,0},{8,4},{4,8},{0,12},{13,1},{9,5},{5,9},{1,13},{14,2},{10,6},... | collective-permute-start | bytes 98312 | tf_op jit(solution)/shard_map/ppermute | solution.py:52
  5.0 4.9 %collective-permute-start.1 = (bf16[128,128]{1,0:T(8,128)(2,1)S(1)}, bf16[128,128]{1,0:T(8,128)(2,1)S(1)}, u32[]{:S(2)}, u32[]{:S(2)}) collective-permute-start(bf16[128,128]{1,0:T(8,128)(2,1)S(1)} %get-tuple-element.13.after_ref.refs_0_), channel_id=1, source_target_pairs={{8,0},{12,4},{0,8},{4,12},{9,1},{13,5},{1,9},{5,13},{10,2},{14,6},... | collective-permute-start | bytes 98312 | tf_op jit(solution)/shard_map/ppermute | solution.py:52
  5.6 4.4 %collective-permute-start = (bf16[128,128]{1,0:T(8,128)(2,1)S(1)}, bf16[128,128]{1,0:T(8,128)(2,1)S(1)}, u32[]{:S(2)}, u32[]{:S(2)}) collective-permute-start(bf16[128,128]{1,0:T(8,128)(2,1)S(1)} %get-tuple-element.13.after_ref.refs_0_), channel_id=1, source_target_pairs={{4,0},{0,4},{12,8},{8,12},{5,1},{1,5},{13,9},{9,13},{6,2},{2,6},{1... | collective-permute-start | bytes 98312 | tf_op jit(solution)/shard_map/ppermute | solution.py:52
  10.2 1.6 %collective-permute-start.3 = (f32[2,264,128]{2,1,0:T(8,128)S(1)}, f32[2,264,128]{2,1,0:T(8,128)S(1)}, u32[]{:S(2)}, u32[]{:S(2)}) collective-permute-start(f32[2,264,128]{2,1,0:T(8,128)S(1)} %first.1.after_ref.mine_ref), channel_id=1, source_target_pairs={{0,16},{16,0},{1,17},{17,1},{2,18},{18,2},{3,19},{19,3},{4,20},{20... | collective-permute-start | bytes 811016 | tf_op jit(solution)/shard_map/ppermute | solution.py:65
  11.9 5.9 %collective-permute-start.5 = (bf16[2,128,128]{2,1,0:T(8,128)(2,1)S(1)}, bf16[2,128,128]{2,1,0:T(8,128)(2,1)S(1)}, u32[]{:S(2)}, u32[]{:S(2)}) collective-permute-start(bf16[2,128,128]{2,1,0:T(8,128)(2,1)S(1)} %get-tuple-element.20), channel_id=1, source_target_pairs={{8,0},{12,4},{0,8},{4,12},{28,16},{24,20},{20,24},{16,28},{9,1},{1... | collective-permute-start | bytes 196616 | tf_op jit(solution)/shard_map/ppermute | solution.py:61
  13.9 3.9 %collective-permute-start.4 = (bf16[128,128]{1,0:T(8,128)(2,1)S(1)}, bf16[128,128]{1,0:T(8,128)(2,1)S(1)}, u32[]{:S(2)}, u32[]{:S(2)}) collective-permute-start(bf16[128,128]{1,0:T(8,128)(2,1)S(1)} %get-tuple-element.19.after_ref.refs_0_.refs_1_), channel_id=1, source_target_pairs={{4,0},{0,4},{12,8},{8,12},{5,1},{1,5},{13,9},{9,13},{6,2},{2,6},{1... | collective-permute-start | bytes 98312 | tf_op jit(solution)/shard_map/ppermute | solution.py:52
  18.0 1.3 %collective-permute-start.6 = (f32[128,128]{1,0:T(8,128)S(1)}, f32[128,128]{1,0:T(8,128)S(1)}, u32[]{:S(2)}, u32[]{:S(2)}) collective-permute-start(f32[128,128]{1,0:T(8,128)S(1)} %second.2.refs_0_), channel_id=1, source_target_pairs={{0,16},{16,0},{1,17},{17,1},{2,18},{18,2},{3,19},{19,3},{4,20},{20... | collective-permute-start | bytes 196616 | tf_op jit(solution)/shard_map/ppermute | solution.py:65
where the time goes:
time: 20 us
  starting transfers between devices  8.01 us (40%)
  Pallas kernels  6.3 us (32%)
  waiting for transfers between devices  4.88 us (24%)
  between operations  0.77 us (4%)
    ppermute x4, starting transfers between devices, from_column(): lax.ppermute(value, 'col', [(partner(col, offset, cols), col) for col in...  5.89 us
    pallas_call x1, Pallas kernels, local(): call(functools.partial(sum_kernel, rows, cols, owned_blocks), [jax.ShapeD...  3.58 us
    ppermute x4, waiting for transfers between devices, from_column(): lax.ppermute(value, 'col', [(partner(col, offset, cols), col) for col in...  2.61 us
    ppermute x2, waiting for transfers between devices, swap_rows(): return lax.ppermute(value, 'row', [(0, 1), (1, 0)])  2.27 us
    ppermute x1, starting transfers between devices, from_hop(): return lax.ppermute(value, ('row', 'col'), pairs)  1.98 us
    pallas_call x1, Pallas kernels, local(): call(scale_kernel, [jax.ShapeDtypeStruct((sets, owned), low), pltpu.SMEM(...  1.07 us
    pallas_call x1, Pallas kernels, finish(): call(functools.partial(finish_kernel, last), piece if last else jax.Shape...  0.65 us
    pallas_call x2, Pallas kernels, second(): call(functools.partial(second_kernel, place, len(after)), piece, 'second'...  0.4 us
  transfers between devices with their start and end apart: 7, of which 3 were waited for; matrix products, arithmetic and copies ran while one was open for 0% of the time, Pallas kernels for 20%

commit v1 on v0

--- a/solution.py
+++ b/solution.py
@@ -20,7 +20,7 @@
 
 TILES_VMEM = 32 * 1024 * 1024
 SMALL_VMEM = 8 * 1024 * 1024
-LANES = 4
+STRIPS = 4
 UNROLL = 8
 DEGREE_LINES = 8
 
@@ -90,16 +90,17 @@
 def sum_kernel(
     rows, cols, owned_blocks, after_ref, count_ref, out_ref, in_ref, tiles_ref, *rest
 ):
-    *weight_refs, total = rest
+    weight_refs, totals = rest[:rows], rest[rows:]
     in_blocks = cols * owned_blocks
     slots, edge = tiles_ref.shape[2], tiles_ref.shape[3]
     owned = owned_blocks * edge
-    spare = total.shape[1] - 1
+    spare, strip = totals[0].shape[0] - 1, totals[0].shape[1]
     unroll = math.gcd(slots, UNROLL)
     row = lax.axis_index("row")
     occupied = count_ref[0, 0]
 
-    total[...] = jnp.zeros(total.shape, jnp.float32)
+    for total in totals:
+        total[...] = jnp.zeros(total.shape, jnp.float32)
 
     def add_tiles(step, carry):
         at = step * unroll
@@ -107,14 +108,11 @@
         for lane in range(unroll):
             slot = at + lane
             pair = out_ref[0, 0, slot] * in_blocks + in_ref[0, 0, slot]
-            places.append((lane % LANES, jnp.where(slot < occupied, pair, spare), slot))
-        for start in range(0, unroll, 2):
-            sums = [
-                (lane, pair, total[lane, pair] + tiles_ref[0, 0, slot].astype(jnp.float32))
-                for lane, pair, slot in places[start:start + 2]
-            ]
-            for lane, pair, value in sums:
-                total[lane, pair] = value
+            places.append((slot, jnp.where(slot < occupied, pair, spare)))
+        for slot, pair in places:
+            for index, total in enumerate(totals):
+                lines = slice(index * strip, (index + 1) * strip)
+                total[pair] += tiles_ref[0, 0, slot, lines].astype(jnp.float32)
         return carry
 
     lax.fori_loop(0, (occupied + unroll - 1) // unroll, add_tiles, 0)
@@ -125,13 +123,14 @@
             columns = slice(block * edge, (block + 1) * edge)
             for source in range(in_blocks):
                 pair = (owner * owned_blocks + block) * in_blocks + source
-                value = (total[0, pair] + total[1, pair]) + (total[2, pair] + total[3, pair])
-                high = value.astype(jnp.bfloat16)
-                low = (value - high.astype(jnp.float32)).astype(jnp.bfloat16)
-                column, line = source // owned_blocks, source % owned_blocks * edge
-                lines = slice(line, line + edge)
-                weight_refs[place][column, lines, columns] = high
-                weight_refs[place][column, lines, owned + block * edge:owned + (block + 1) * edge] = low
+                for index, total in enumerate(totals):
+                    value = total[pair]
+                    high = value.astype(jnp.bfloat16)
+                    low = (value - high.astype(jnp.float32)).astype(jnp.bfloat16)
+                    column, line = source // owned_blocks, source % owned_blocks * edge + index * strip
+                    lines = slice(line, line + strip)
+                    weight_refs[place][column, lines, columns] = high
+                    weight_refs[place][column, lines, owned + block * edge:owned + (block + 1) * edge] = low
 
 
 def times_weight(parts, weights):
@@ -266,7 +265,7 @@
         "sum_tiles",
         in_specs=[ANY] + [SMEM] * 3 + [VMEM],
         out_specs=[VMEM] * rows,
-        scratch_shapes=[pltpu.VMEM((LANES, out_blocks * in_blocks + 1, edge, edge), jnp.float32)],
+        scratch_shapes=[pltpu.VMEM((out_blocks * in_blocks + 1, edge // STRIPS, edge), jnp.float32)] * STRIPS,
         vmem=TILES_VMEM,
         flops=slots * edge * edge,
         size=2 * slots * edge * edge,

time: 20 us -> 19.2 us (0.960)
  waiting for transfers between devices: 4.88 us -> 7.73 us
  Pallas kernels: 6.3 us -> 3.71 us
  starting transfers between devices: 8.01 us -> 6.86 us
    ppermute x4, waiting for transfers between devices: 2.61 us -> 5.46 us  [from_column(): lax.ppermute(value, 'col', [(partner(col, offset, cols), col) for col in...]
    pallas_call x1, Pallas kernels: 3.58 us -> 0.99 us  [local(): call(functools.partial(sum_kernel, rows, cols, owned_blocks), [jax.ShapeD...]
    ppermute x4, starting transfers between devices: 5.89 us -> 5.14 us  [from_column(): lax.ppermute(value, 'col', [(partner(col, offset, cols), col) for col in...]
    ppermute x1, starting transfers between devices: 1.98 us -> 1.58 us  [from_hop(): return lax.ppermute(value, ('row', 'col'), pairs)]
  transfers between devices with their start and end apart: 7 -> 7, of which waited for: 3 -> 5; matrix products, arithmetic and copies ran while one was open for 0% -> 0% of each run, Pallas kernels for 20% -> 8%
where the time goes in v1:
time: 19.2 us; the launch traced here: 19.1 us
  waiting for transfers between devices  7.73 us (40%)
  starting transfers between devices  6.86 us (36%)
  Pallas kernels  3.71 us (19%)
  between operations  0.74 us (4%)
    ppermute x4, waiting for transfers between devices, from_column(): lax.ppermute(value, 'col', [(partner(col, offset, cols), col) for col in...  5.46 us
    ppermute x4, starting transfers between devices, from_column(): lax.ppermute(value, 'col', [(partner(col, offset, cols), col) for col in...  5.14 us
    ppermute x2, waiting for transfers between devices, swap_rows(): return lax.ppermute(value, 'row', [(0, 1), (1, 0)])  2.27 us
    ppermute x1, starting transfers between devices, from_hop(): return lax.ppermute(value, ('row', 'col'), pairs)  1.58 us
    pallas_call x1, Pallas kernels, local(): call(scale_kernel, [jax.ShapeDtypeStruct((sets, owned), low), pltpu.SMEM(...  1.07 us
    pallas_call x1, Pallas kernels, local(): call(functools.partial(sum_kernel, rows, cols, owned_blocks), [jax.ShapeD...  0.99 us
    pallas_call x1, Pallas kernels, finish(): call(functools.partial(finish_kernel, last), piece if last else jax.Shape...  0.65 us
    pallas_call x2, Pallas kernels, second(): call(functools.partial(second_kernel, place, len(after)), piece, 'second'...  0.4 us
  transfers between devices with their start and end apart: 7, of which 5 were waited for; matrix products, arithmetic and copies ran while one was open for 0% of the time, Pallas kernels for 8%

profile of v1, /device:TPU:0, one launch (start us, length us, event | category | flops | bytes accessed | tf_op | source)
XLA Modules:
  0.0 19.1 jit_solution(15616104876406255972)
XLA Ops:
  0.0 0.0 copy-start
  0.0 1.1 %scale.1 = (bf16[128,128]{1,0:T(8,128)(2,1)S(1)}, s32[1,1,384]{2,1,0:T(1,128)S(4)}, s32[1,1,384]{2,1,0:T(1,128)S(4)}, s32[16,128]{1,0:T(8,128)S(1)}) custom-call(f32[128,128]{1,0:T(8,128)} %prior_hbm.1, s32[1,128]{1,0:T(1,128)} %bitcast.2, s32[1,1,384]{2,1,0:T(1,128)} %out_hbm.1, s32[1,1,384]{2,1,0:T(1,128)} %in_hbm.1, s32[16,128]{1,0:T(8,128)} %bitcast.5), custom_call_target="tpu_custom_call" | custom-call | flops 12884901888 | bytes 98304 | tf_op jit(solution)/shard_map/scale/pallas_call | solution.py:237
  1.1 0.0 copy-start.1
  1.1 4.0 %collective-permute-start.2 = (bf16[128,128]{1,0:T(8,128)(2,1)S(1)}, bf16[128,128]{1,0:T(8,128)(2,1)S(1)}, u32[]{:S(2)}, u32[]{:S(2)}) collective-permute-start(bf16[128,128]{1,0:T(8,128)(2,1)S(1)} %get-tuple-element.13.after_ref.refs_0_), channel_id=1, source_target_pairs={{12,0},{8,4},{4,8},{0,12},{13,1},{9,5},{5,9},{1,13},{14,2},{10,6},... | collective-permute-start | bytes 98312 | tf_op jit(solution)/shard_map/ppermute | solution.py:52
  5.0 0.5 %collective-permute-start.1 = (bf16[128,128]{1,0:T(8,128)(2,1)S(1)}, bf16[128,128]{1,0:T(8,128)(2,1)S(1)}, u32[]{:S(2)}, u32[]{:S(2)}) collective-permute-start(bf16[128,128]{1,0:T(8,128)(2,1)S(1)} %get-tuple-element.13.after_ref.refs_0_), channel_id=1, source_target_pairs={{8,0},{12,4},{0,8},{4,12},{9,1},{13,5},{1,9},{5,13},{10,2},{14,6},... | collective-permute-start | bytes 98312 | tf_op jit(solution)/shard_map/ppermute | solution.py:52
  5.6 0.1 collective-permute-start
  6.3 0.0 copy-done
  6.4 1.0 %sum_tiles.1 = (bf16[4,128,256]{2,1,0:T(8,128)(2,1)S(1)}, bf16[4,128,256]{2,1,0:T(8,128)(2,1)S(1)}) custom-call(bf16[128,128]{1,0:T(8,128)(2,1)S(1)} %get-tuple-element.13.after_ref.refs_0_, s32[1,1]{1,0:T(1,128)S(6)} %copy.8.count_ref, s32[1,1,384]{2,1,0:T(1,128)S(4)} %get-tuple-element.14.out_ref, s32[1,1,384]{2,1,0:T(1,128)S(4)} %get-tuple-element.15.in_ref, ...), custom_call_target="tpu_custom_call" | custom-call | flops 6291456 | bytes 12582912 | tf_op jit(solution)/shard_map/sum_tiles/pallas_call | solution.py:262
  7.4 0.0 collective-permute-done.2.refs_3_
  7.4 1.6 %collective-permute-done.1.refs_2_ = bf16[128,128]{1,0:T(8,128)(2,1)S(1)} collective-permute-done((bf16[128,128]{1,0:T(8,128)(2,1)S(1)}, bf16[128,128]{1,0:T(8,128)(2,1)S(1)}, u32[]{:S(2)}, u32[]{:S(2)}) %collective-permute-start.1) | collective-permute-done | bytes 32800 | tf_op jit(solution)/shard_map/ppermute | solution.py:52
  9.0 0.5 %collective-permute-done.refs_1_ = bf16[128,128]{1,0:T(8,128)(2,1)S(1)} collective-permute-done((bf16[128,128]{1,0:T(8,128)(2,1)S(1)}, bf16[128,128]{1,0:T(8,128)(2,1)S(1)}, u32[]{:S(2)}, u32[]{:S(2)}) %collective-permute-start) | collective-permute-done | bytes 32800 | tf_op jit(solution)/shard_map/ppermute | solution.py:52
  9.5 0.0 copy-done.1
  9.5 0.2 %first.1.after_ref.mine_ref = f32[2,264,128]{2,1,0:T(8,128)S(1)} custom-call(bf16[128,128]{1,0:T(8,128)(2,1)S(1)} %get-tuple-element.13.after_ref.refs_0_, bf16[128,128]{1,0:T(8,128)(2,1)S(1)} %collective-permute-done.refs_1_, bf16[128,128]{1,0:T(8,128)(2,1)S(1)} %collective-permute-done.1.refs_2_, bf16[128,128]{1,0:T(8,128)(2,1)S(1)} %collective-permute-done.2.refs_3_, ...), custom_call_target="tpu_custom_call" | custom-call | flops 67108864 | bytes 524288 | tf_op jit(solution)/shard_map/first/pallas_call | solution.py:309
  9.7 0.1 collective-permute-start.3
  9.8 0.3 %restart.1.restart_ref.refs_2_ = f32[2,128,128]{2,1,0:T(8,128)S(1)} custom-call(f32[2,264,128]{2,1,0:T(8,128)S(1)} %first.1.after_ref.mine_ref, s32[16,128]{1,0:T(8,128)S(1)} %get-tuple-element.18.seeds_ref), custom_call_target="tpu_custom_call" | custom-call | flops 1048576 | bytes 131072 | tf_op jit(solution)/shard_map/restart/pallas_call | solution.py:288
  10.1 1.2 %collective-permute-done.3.theirs_ref = f32[2,264,128]{2,1,0:T(8,128)S(1)} collective-permute-done((f32[2,264,128]{2,1,0:T(8,128)S(1)}, f32[2,264,128]{2,1,0:T(8,128)S(1)}, u32[]{:S(2)}, u32[]{:S(2)}) %collective-permute-start.3) | collective-permute-done | bytes 270368 | tf_op jit(solution)/shard_map/ppermute | solution.py:65
  11.4 1.6 %collective-permute-start.5 = (bf16[2,128,128]{2,1,0:T(8,128)(2,1)S(1)}, bf16[2,128,128]{2,1,0:T(8,128)(2,1)S(1)}, u32[]{:S(2)}, u32[]{:S(2)}) collective-permute-start(bf16[2,128,128]{2,1,0:T(8,128)(2,1)S(1)} %get-tuple-element.20), channel_id=1, source_target_pairs={{8,0},{12,4},{0,8},{4,12},{28,16},{24,20},{20,24},{16,28},{9,1},{1... | collective-permute-start | bytes 196616 | tf_op jit(solution)/shard_map/ppermute | solution.py:61
  13.0 0.5 %collective-permute-start.4 = (bf16[128,128]{1,0:T(8,128)(2,1)S(1)}, bf16[128,128]{1,0:T(8,128)(2,1)S(1)}, u32[]{:S(2)}, u32[]{:S(2)}) collective-permute-start(bf16[128,128]{1,0:T(8,128)(2,1)S(1)} %get-tuple-element.19.after_ref.refs_0_.refs_1_), channel_id=1, source_target_pairs={{4,0},{0,4},{12,8},{8,12},{5,1},{1,5},{13,9},{9,13},{6,2},{2,6},{1... | collective-permute-start | bytes 98312 | tf_op jit(solution)/shard_map/ppermute | solution.py:52
  13.5 3.4 %collective-permute-done.4.refs_1_.refs_2_ = bf16[128,128]{1,0:T(8,128)(2,1)S(1)} collective-permute-done((bf16[128,128]{1,0:T(8,128)(2,1)S(1)}, bf16[128,128]{1,0:T(8,128)(2,1)S(1)}, u32[]{:S(2)}, u32[]{:S(2)}) %collective-permute-start.4) | collective-permute-done | bytes 32800 | tf_op jit(solution)/shard_map/ppermute | solution.py:52
  16.9 0.0 collective-permute-done.5.refs_2_.refs_3_
  16.9 0.2 %second.2.refs_0_ = f32[128,128]{1,0:T(8,128)S(1)} custom-call(bf16[128,128]{1,0:T(8,128)(2,1)S(1)} %get-tuple-element.19.after_ref.refs_0_.refs_1_, bf16[128,128]{1,0:T(8,128)(2,1)S(1)} %collective-permute-done.4.refs_1_.refs_2_, bf16[2,128,128]{2,1,0:T(8,128)(2,1)S(1)} %collective-permute-done.5.refs_2_.refs_3_, ...), custom_call_target="tpu_custom_call" | custom-call | flops 33554432 | bytes 262144 | tf_op jit(solution)/shard_map/second/pallas_call | solution.py:340
  17.1 0.1 collective-permute-start.6
  17.2 0.2 %second.3.refs_0_ = f32[128,128]{1,0:T(8,128)S(1)} custom-call(f32[128,128]{1,0:T(8,128)S(1)} %second.2.refs_0_, bf16[128,128]{1,0:T(8,128)(2,1)S(1)} %get-tuple-element.19.after_ref.refs_0_.refs_1_, bf16[128,128]{1,0:T(8,128)(2,1)S(1)} %collective-permute-done.4.refs_1_.refs_2_, bf16[2,128,128]{2,1,0:T(8,128)(2,1)S(1)} %collective-permute-done.5.refs_2_.refs_3_, ...), custom_call_target="tpu_custom_call" | custom-call | flops 33554432 | bytes 262144 | tf_op jit(solution)/shard_map/second/pallas_call | solution.py:340
  17.4 1.0 %collective-permute-done.6.refs_1_ = f32[128,128]{1,0:T(8,128)S(1)} collective-permute-done((f32[128,128]{1,0:T(8,128)S(1)}, f32[128,128]{1,0:T(8,128)S(1)}, u32[]{:S(2)}, u32[]{:S(2)}) %collective-permute-start.6) | collective-permute-done | bytes 65568 | tf_op jit(solution)/shard_map/ppermute | solution.py:65
  18.4 0.7 %last.1 = f32[128,128]{1,0:T(8,128)} custom-call(f32[128,128]{1,0:T(8,128)S(1)} %second.3.refs_0_, f32[128,128]{1,0:T(8,128)S(1)} %collective-permute-done.6.refs_1_, f32[2,128,128]{2,1,0:T(8,128)S(1)} %restart.1.restart_ref.refs_2_, s32[1,128]{1,0:T(1,128)S(1)} %bitcast.4), custom_call_target="tpu_custom_call" | custom-call | bytes 196608 | tf_op jit(solution)/shard_map/last/pallas_call | solution.py:299
  (2 shorter events, 0.1 us)
Async XLA Ops:
  0.0 6.3 %copy-start = (bf16[1,1,384,128,128]{4,3,2,1,0:T(8,128)(2,1)S(1)}, bf16[1,1,384,128,128]{4,3,2,1,0:T(8,128)(2,1)}, u32[]{:S(2)}) copy-start(bf16[1,1,384,128,128]{4,3,2,1,0:T(8,128)(2,1)} %tiles_ref.1) | copy-start | bytes 37748740
  1.1 8.4 %copy-start.1 = (s32[128]{0:T(128)S(1)}, s32[128]{0:T(128)}, u32[]{:S(2)}) copy-start(s32[128]{0:T(128)} %param.11) | copy-start | bytes 1540
  1.1 6.3 %collective-permute-start.2 = (bf16[128,128]{1,0:T(8,128)(2,1)S(1)}, bf16[128,128]{1,0:T(8,128)(2,1)S(1)}, u32[]{:S(2)}, u32[]{:S(2)}) collective-permute-start(bf16[128,128]{1,0:T(8,128)(2,1)S(1)} %get-tuple-element.13.after_ref.refs_0_), channel_id=1, source_target_pairs={{12,0},{8,4},{4,8},{0,12},{13,1},{9,5},{5,9},{1,13},{14,2},{10,6},... | collective-permute-start | bytes 98312 | tf_op jit(solution)/shard_map/ppermute | solution.py:52
  5.0 3.9 %collective-permute-start.1 = (bf16[128,128]{1,0:T(8,128)(2,1)S(1)}, bf16[128,128]{1,0:T(8,128)(2,1)S(1)}, u32[]{:S(2)}, u32[]{:S(2)}) collective-permute-start(bf16[128,128]{1,0:T(8,128)(2,1)S(1)} %get-tuple-element.13.after_ref.refs_0_), channel_id=1, source_target_pairs={{8,0},{12,4},{0,8},{4,12},{9,1},{13,5},{1,9},{5,13},{10,2},{14,6},... | collective-permute-start | bytes 98312 | tf_op jit(solution)/shard_map/ppermute | solution.py:52
  5.6 3.9 %collective-permute-start = (bf16[128,128]{1,0:T(8,128)(2,1)S(1)}, bf16[128,128]{1,0:T(8,128)(2,1)S(1)}, u32[]{:S(2)}, u32[]{:S(2)}) collective-permute-start(bf16[128,128]{1,0:T(8,128)(2,1)S(1)} %get-tuple-element.13.after_ref.refs_0_), channel_id=1, source_target_pairs={{4,0},{0,4},{12,8},{8,12},{5,1},{1,5},{13,9},{9,13},{6,2},{2,6},{1... | collective-permute-start | bytes 98312 | tf_op jit(solution)/shard_map/ppermute | solution.py:52
  9.7 1.6 %collective-permute-start.3 = (f32[2,264,128]{2,1,0:T(8,128)S(1)}, f32[2,264,128]{2,1,0:T(8,128)S(1)}, u32[]{:S(2)}, u32[]{:S(2)}) collective-permute-start(f32[2,264,128]{2,1,0:T(8,128)S(1)} %first.1.after_ref.mine_ref), channel_id=1, source_target_pairs={{0,16},{16,0},{1,17},{17,1},{2,18},{18,2},{3,19},{19,3},{4,20},{20... | collective-permute-start | bytes 811016 | tf_op jit(solution)/shard_map/ppermute | solution.py:65
  11.4 5.5 %collective-permute-start.5 = (bf16[2,128,128]{2,1,0:T(8,128)(2,1)S(1)}, bf16[2,128,128]{2,1,0:T(8,128)(2,1)S(1)}, u32[]{:S(2)}, u32[]{:S(2)}) collective-permute-start(bf16[2,128,128]{2,1,0:T(8,128)(2,1)S(1)} %get-tuple-element.20), channel_id=1, source_target_pairs={{8,0},{12,4},{0,8},{4,12},{28,16},{24,20},{20,24},{16,28},{9,1},{1... | collective-permute-start | bytes 196616 | tf_op jit(solution)/shard_map/ppermute | solution.py:61
  13.0 3.9 %collective-permute-start.4 = (bf16[128,128]{1,0:T(8,128)(2,1)S(1)}, bf16[128,128]{1,0:T(8,128)(2,1)S(1)}, u32[]{:S(2)}, u32[]{:S(2)}) collective-permute-start(bf16[128,128]{1,0:T(8,128)(2,1)S(1)} %get-tuple-element.19.after_ref.refs_0_.refs_1_), channel_id=1, source_target_pairs={{4,0},{0,4},{12,8},{8,12},{5,1},{1,5},{13,9},{9,13},{6,2},{2,6},{1... | collective-permute-start | bytes 98312 | tf_op jit(solution)/shard_map/ppermute | solution.py:52
  17.1 1.3 %collective-permute-start.6 = (f32[128,128]{1,0:T(8,128)S(1)}, f32[128,128]{1,0:T(8,128)S(1)}, u32[]{:S(2)}, u32[]{:S(2)}) collective-permute-start(f32[128,128]{1,0:T(8,128)S(1)} %second.2.refs_0_), channel_id=1, source_target_pairs={{0,16},{16,0},{1,17},{17,1},{2,18},{18,2},{3,19},{19,3},{4,20},{20... | collective-permute-start | bytes 196616 | tf_op jit(solution)/shard_map/ppermute | solution.py:65

commit v2 on v1

--- a/solution.py
+++ b/solution.py
@@ -21,7 +21,7 @@
 TILES_VMEM = 32 * 1024 * 1024
 SMALL_VMEM = 8 * 1024 * 1024
 STRIPS = 4
-UNROLL = 8
+UNROLL = 32
 DEGREE_LINES = 8
 
 
@@ -61,30 +61,25 @@
     return lax.ppermute(value, ("row", "col"), pairs)
 
 
+def from_side(value, cols):
+    pairs = [((1 - row) * cols + (col ^ 1), row * cols + col) for row in range(2) for col in range(cols)]
+    return lax.ppermute(value, ("row", "col"), pairs)
+
+
 def swap_rows(value):
     return lax.ppermute(value, "row", [(0, 1), (1, 0)])
 
 
-def scale_kernel(
-    prior_hbm, degree_hbm, out_hbm, in_hbm, seeds_hbm,
-    scaled_ref, out_ref, in_ref, seeds_ref, prior_ref, degree_ref, arrived,
-):
-    moves = (
-        (prior_hbm, prior_ref), (degree_hbm, degree_ref),
-        (out_hbm, out_ref), (in_hbm, in_ref), (seeds_hbm, seeds_ref),
-    )
+def scale_kernel(prior_hbm, degree_hbm, scaled_ref, prior_ref, degree_ref, arrived):
     copies = [
         pltpu.make_async_copy(source, place, arrived.at[index])
-        for index, (source, place) in enumerate(moves)
+        for index, (source, place) in enumerate(((prior_hbm, prior_ref), (degree_hbm, degree_ref)))
     ]
     for copy in copies:
         copy.start()
-    for copy in copies[:2]:
+    for copy in copies:
         copy.wait()
-    scaled = (prior_ref[...] / degree_ref[...].astype(jnp.float32)).astype(jnp.bfloat16)
-    scaled_ref[...] = scaled
-    for copy in copies[2:]:
-        copy.wait()
+    scaled_ref[...] = (prior_ref[...] / degree_ref[...].astype(jnp.float32)).astype(jnp.bfloat16)
 
 
 def sum_kernel(
@@ -186,7 +181,7 @@
         )
 
 
-def both_kernel(mine_ref, theirs_ref, restart_ref, own_ref, scaled_ref):
+def both_kernel(mine_ref, theirs_ref, restart_ref, other_ref, scaled_ref):
     _, sets, owned = restart_ref.shape
     for place in range(2):
         incoming = mine_ref[place, :sets] + theirs_ref[1 - place, :sets]
@@ -194,8 +189,8 @@
         risk = restart_ref[place] + damping * incoming
         scaled = (risk / degree).astype(jnp.bfloat16)
         scaled_ref[place] = scaled
-        if not place:
-            own_ref[...] = scaled
+        if place:
+            other_ref[...] = scaled
 
 
 def foreign_kernel(after_ref, theirs_ref, weight_ref):
@@ -209,9 +204,9 @@
 
 
 def second_kernel(place, after, *refs):
-    own_ref, side_ref, hop_ref, weight_ref, foreign_ref, result_ref = refs[after:]
+    both_ref, side_ref, hop_ref, weight_ref, foreign_ref, result_ref = refs[after:]
     row, col = lax.axis_index("row"), lax.axis_index("col")
-    parts = [own_ref[...], side_ref[...], hop_ref[0], hop_ref[1]]
+    parts = [both_ref[0], side_ref[...], hop_ref[0], hop_ref[1]]
     weights = [weight_ref[col], weight_ref[col ^ 1], weight_ref[col ^ hop(row)], foreign_ref[place]]
     result_ref[...] = times_weight(parts, weights)
 
@@ -234,25 +229,20 @@
     degree = out_degree.reshape(1, owned)
     low = jnp.bfloat16
 
-    scaled, out_ids, in_ids, seeds = call(
+    scaled = call(
         scale_kernel,
-        [
-            jax.ShapeDtypeStruct((sets, owned), low),
-            pltpu.SMEM(tile_out.shape, jnp.int32),
-            pltpu.SMEM(tile_in.shape, jnp.int32),
-            jax.ShapeDtypeStruct((seed_ids.shape[1], sets), jnp.int32),
-        ],
+        jax.ShapeDtypeStruct((sets, owned), low),
         "scale",
-        in_specs=[HBM] * 5,
-        out_specs=[VMEM, SMEM, SMEM, VMEM],
+        in_specs=[HBM] * 2,
+        out_specs=VMEM,
         scratch_shapes=[
             pltpu.VMEM((sets, owned), jnp.float32),
             pltpu.VMEM((1, owned), jnp.int32),
-            pltpu.SemaphoreType.DMA((5,)),
+            pltpu.SemaphoreType.DMA((2,)),
         ],
         flops=16 * slots * edge**3,
         size=6 * sets * owned,
-    )(*in_hbm(prior, degree, tile_out, tile_in, seed_ids.T))
+    )(*in_hbm(prior, degree))
 
     def spread(value):
         return [from_column(value, cols, offset) if offset else value for offset in range(cols)]
@@ -269,7 +259,7 @@
         vmem=TILES_VMEM,
         flops=slots * edge * edge,
         size=2 * slots * edge * edge,
-    )(scaled, tile_count, out_ids, in_ids, tiles)
+    )(scaled, tile_count, tile_out, tile_in, tiles)
 
     piece = jax.ShapeDtypeStruct((sets, owned), jnp.float32)
 
@@ -293,7 +283,7 @@
             out_specs=VMEM,
             flops=2 * places * sets * owned * seed_ids.shape[1],
             size=4 * places * sets * owned,
-        )(after, seeds)
+        )(after, seed_ids.T)
 
     def finish(incoming, restart, last):
         return call(
@@ -317,7 +307,7 @@
         )(*parts, *weights, degree)
         theirs = swap_rows(mine)
         restart = count_restart(2, mine)
-        own, both = call(
+        other, both = call(
             both_kernel,
             [jax.ShapeDtypeStruct((sets, owned), low), jax.ShapeDtypeStruct((2, sets, owned), low)],
             "both",
@@ -325,7 +315,7 @@
             out_specs=[VMEM] * 2,
             size=24 * sets * owned,
         )(mine, theirs, restart)
-        side = from_column(own, cols, 1)
+        side = from_side(other, cols)
         near = from_hop(both, cols)
         foreign = call(
             foreign_kernel,
@@ -334,7 +324,7 @@
             in_specs=[ANY, VMEM],
             out_specs=VMEM,
             size=16 * owned * owned,
-        )(own, theirs)
+        )(other, theirs)
 
         def second(place, *after):
             return call(
@@ -345,7 +335,7 @@
                 out_specs=VMEM,
                 flops=4 * sets * cols * owned * owned,
                 size=4 * cols * owned * owned,
-            )(*after, own, side, near, weights[place], foreign)
+            )(*after, both, side, near, weights[place], foreign)
 
         leaving = second(1)
         received = swap_rows(leaving)

time: 19.2 us -> 18.9 us (0.984)
  waiting for transfers between devices: 7.73 us -> 6.63 us
  starting transfers between devices: 6.86 us -> 7.37 us
  Pallas kernels: 3.71 us -> 4.01 us
    ppermute x4 -> x3, waiting for transfers between devices: 5.46 us -> 1.73 us  [from_column(): lax.ppermute(value, 'col', [(partner(col, offset, cols), col) for col in...]
    ppermute x0 -> x1, waiting for transfers between devices: none -> 2.73 us  [from_side(): return lax.ppermute(value, ('row', 'col'), pairs)]
    ppermute x0 -> x1, starting transfers between devices: none -> 0.92 us  [from_side(): return lax.ppermute(value, ('row', 'col'), pairs)]
    ppermute x4 -> x3, starting transfers between devices: 5.14 us -> 4.61 us  [from_column(): lax.ppermute(value, 'col', [(partner(col, offset, cols), col) for col in...]
    pallas_call x1, Pallas kernels: 0.99 us -> 1.35 us  [local(): call(functools.partial(sum_kernel, rows, cols, owned_blocks), [jax.ShapeD...]
  transfers between devices with their start and end apart: 7 -> 7, of which waited for: 5 -> 5; matrix products, arithmetic and copies ran while one was open for 0% -> 0% of each run, Pallas kernels for 8% -> 10%
where the time goes in v2:
time: 18.9 us; the launch traced here: 18.8 us
  starting transfers between devices  7.37 us (39%)
  waiting for transfers between devices  6.63 us (35%)
  Pallas kernels  4.01 us (21%)
  between operations  0.76 us (4%)
    ppermute x3, starting transfers between devices, from_column(): lax.ppermute(value, 'col', [(partner(col, offset, cols), col) for col in...  4.61 us
    ppermute x1, waiting for transfers between devices, from_side(): return lax.ppermute(value, ('row', 'col'), pairs)  2.73 us
    ppermute x2, waiting for transfers between devices, swap_rows(): return lax.ppermute(value, 'row', [(0, 1), (1, 0)])  2.17 us
    ppermute x3, waiting for transfers between devices, from_column(): lax.ppermute(value, 'col', [(partner(col, offset, cols), col) for col in...  1.73 us
    ppermute x1, starting transfers between devices, from_hop(): return lax.ppermute(value, ('row', 'col'), pairs)  1.58 us
    pallas_call x1, Pallas kernels, local(): call(functools.partial(sum_kernel, rows, cols, owned_blocks), [jax.ShapeD...  1.35 us
    pallas_call x1, Pallas kernels, local(): call(scale_kernel, jax.ShapeDtypeStruct((sets, owned), low), 'scale', in_...  1.02 us
    ppermute x1, starting transfers between devices, from_side(): return lax.ppermute(value, ('row', 'col'), pairs)  0.92 us
  transfers between devices with their start and end apart: 7, of which 5 were waited for; matrix products, arithmetic and copies ran while one was open for 0% of the time, Pallas kernels for 10%

profile of v2, /device:TPU:0, one launch (start us, length us, event | category | flops | bytes accessed | tf_op | source)
XLA Modules:
  0.0 18.8 jit_solution(16322535590757858523)
XLA Ops:
  0.0 0.0 copy-start
  0.0 0.0 copy-start.3
  0.0 0.0 copy-start.4
  0.0 1.0 %scale.1.after_ref.refs_0_ = bf16[128,128]{1,0:T(8,128)(2,1)S(1)} custom-call(f32[128,128]{1,0:T(8,128)} %prior_hbm.1, s32[1,128]{1,0:T(1,128)} %bitcast.3), custom_call_target="tpu_custom_call" | custom-call | flops 12884901888 | bytes 98304 | tf_op jit(solution)/shard_map/scale/pallas_call | solution.py:232
  1.0 0.0 copy-start.2
  1.0 0.0 copy-start.1
  1.1 4.0 %collective-permute-start.2 = (bf16[128,128]{1,0:T(8,128)(2,1)S(1)}, bf16[128,128]{1,0:T(8,128)(2,1)S(1)}, u32[]{:S(2)}, u32[]{:S(2)}) collective-permute-start(bf16[128,128]{1,0:T(8,128)(2,1)S(1)} %scale.1.after_ref.refs_0_), channel_id=1, source_target_pairs={{12,0},{8,4},{4,8},{0,12},{13,1},{9,5},{5,9},{1,13},{14,2},{10,6},... | collective-permute-start | bytes 98312 | tf_op jit(solution)/shard_map/ppermute | solution.py:52
  5.0 0.5 %collective-permute-start.1 = (bf16[128,128]{1,0:T(8,128)(2,1)S(1)}, bf16[128,128]{1,0:T(8,128)(2,1)S(1)}, u32[]{:S(2)}, u32[]{:S(2)}) collective-permute-start(bf16[128,128]{1,0:T(8,128)(2,1)S(1)} %scale.1.after_ref.refs_0_), channel_id=1, source_target_pairs={{8,0},{12,4},{0,8},{4,12},{9,1},{13,5},{1,9},{5,13},{10,2},{14,6},... | collective-permute-start | bytes 98312 | tf_op jit(solution)/shard_map/ppermute | solution.py:52
  5.5 0.1 collective-permute-start
  6.3 0.0 copy-done
  6.3 0.0 copy-done.3
  6.3 0.0 copy-done.4
  6.3 1.4 %sum_tiles.1 = (bf16[4,128,256]{2,1,0:T(8,128)(2,1)S(1)}, bf16[4,128,256]{2,1,0:T(8,128)(2,1)S(1)}) custom-call(bf16[128,128]{1,0:T(8,128)(2,1)S(1)} %scale.1.after_ref.refs_0_, s32[1,1]{1,0:T(1,128)S(6)} %copy.8.count_ref, s32[1,1,384]{2,1,0:T(1,128)S(1)} %copy-done.3, s32[1,1,384]{2,1,0:T(1,128)S(1)} %copy-done.4, bf16[1,1,384,128,128]{4,3,2,1,0:T(8,128)(2,1)S(1)} %copy-done), custom_call_target="tpu_custom_call" | custom-call | flops 6291456 | bytes 12582912 | tf_op jit(solution)/shard_map/sum_tiles/pallas_call | solution.py:252
  7.7 0.0 collective-permute-done.2.refs_3_
  7.7 1.2 %collective-permute-done.1.refs_2_ = bf16[128,128]{1,0:T(8,128)(2,1)S(1)} collective-permute-done((bf16[128,128]{1,0:T(8,128)(2,1)S(1)}, bf16[128,128]{1,0:T(8,128)(2,1)S(1)}, u32[]{:S(2)}, u32[]{:S(2)}) %collective-permute-start.1) | collective-permute-done | bytes 32800 | tf_op jit(solution)/shard_map/ppermute | solution.py:52
  8.9 0.5 %collective-permute-done.refs_1_ = bf16[128,128]{1,0:T(8,128)(2,1)S(1)} collective-permute-done((bf16[128,128]{1,0:T(8,128)(2,1)S(1)}, bf16[128,128]{1,0:T(8,128)(2,1)S(1)}, u32[]{:S(2)}, u32[]{:S(2)}) %collective-permute-start) | collective-permute-done | bytes 32800 | tf_op jit(solution)/shard_map/ppermute | solution.py:52
  9.4 0.0 copy-done.2
  9.4 0.2 %first.1.after_ref.mine_ref = f32[2,264,128]{2,1,0:T(8,128)S(1)} custom-call(bf16[128,128]{1,0:T(8,128)(2,1)S(1)} %scale.1.after_ref.refs_0_, bf16[128,128]{1,0:T(8,128)(2,1)S(1)} %collective-permute-done.refs_1_, bf16[128,128]{1,0:T(8,128)(2,1)S(1)} %collective-permute-done.1.refs_2_, bf16[128,128]{1,0:T(8,128)(2,1)S(1)} %collective-permute-done.2.refs_3_, ...), custom_call_target="tpu_custom_call" | custom-call | flops 67108864 | bytes 524288 | tf_op jit(solution)/shard_map/first/pallas_call | solution.py:299
  9.7 0.1 collective-permute-start.3
  9.8 0.0 copy-done.1
  9.8 0.3 %restart.1.restart_ref.refs_2_ = f32[2,128,128]{2,1,0:T(8,128)S(1)} custom-call(f32[2,264,128]{2,1,0:T(8,128)S(1)} %first.1.after_ref.mine_ref, s32[16,128]{1,0:T(8,128)S(1)} %bitcast.2), custom_call_target="tpu_custom_call" | custom-call | flops 1048576 | bytes 131072 | tf_op jit(solution)/shard_map/restart/pallas_call | solution.py:278
  10.1 1.2 %collective-permute-done.3.theirs_ref = f32[2,264,128]{2,1,0:T(8,128)S(1)} collective-permute-done((f32[2,264,128]{2,1,0:T(8,128)S(1)}, f32[2,264,128]{2,1,0:T(8,128)S(1)}, u32[]{:S(2)}, u32[]{:S(2)}) %collective-permute-start.3) | collective-permute-done | bytes 270368 | tf_op jit(solution)/shard_map/ppermute | solution.py:70
  11.3 1.6 %collective-permute-start.5 = (bf16[2,128,128]{2,1,0:T(8,128)(2,1)S(1)}, bf16[2,128,128]{2,1,0:T(8,128)(2,1)S(1)}, u32[]{:S(2)}, u32[]{:S(2)}) collective-permute-start(bf16[2,128,128]{2,1,0:T(8,128)(2,1)S(1)} %get-tuple-element.11.refs_0_.refs_1_), channel_id=1, source_target_pairs={{8,0},{12,4},{0,8},{4,12},{28,16},{24,20},{20,24},{16,28},{9,1},{1... | collective-permute-start | bytes 196616 | tf_op jit(solution)/shard_map/ppermute | solution.py:61
  12.9 0.9 %collective-permute-start.4 = (bf16[128,128]{1,0:T(8,128)(2,1)S(1)}, bf16[128,128]{1,0:T(8,128)(2,1)S(1)}, u32[]{:S(2)}, u32[]{:S(2)}) collective-permute-start(bf16[128,128]{1,0:T(8,128)(2,1)S(1)} %get-tuple-element.12.after_ref), channel_id=1, source_target_pairs={{20,0},{16,4},{28,8},{24,12},{4,16},{0,20},{12,24},{8,28},{21,1},{... | collective-permute-start | bytes 98312 | tf_op jit(solution)/shard_map/ppermute | solution.py:66
  13.9 2.7 %collective-permute-done.4.refs_1_.refs_2_ = bf16[128,128]{1,0:T(8,128)(2,1)S(1)} collective-permute-done((bf16[128,128]{1,0:T(8,128)(2,1)S(1)}, bf16[128,128]{1,0:T(8,128)(2,1)S(1)}, u32[]{:S(2)}, u32[]{:S(2)}) %collective-permute-start.4) | collective-permute-done | bytes 32800 | tf_op jit(solution)/shard_map/ppermute | solution.py:66
  16.6 0.0 collective-permute-done.5.refs_2_.refs_3_
  16.6 0.2 %second.2.refs_0_ = f32[128,128]{1,0:T(8,128)S(1)} custom-call(bf16[2,128,128]{2,1,0:T(8,128)(2,1)S(1)} %get-tuple-element.11.refs_0_.refs_1_, bf16[128,128]{1,0:T(8,128)(2,1)S(1)} %collective-permute-done.4.refs_1_.refs_2_, bf16[2,128,128]{2,1,0:T(8,128)(2,1)S(1)} %collective-permute-done.5.refs_2_.refs_3_, ...), custom_call_target="tpu_custom_call" | custom-call | flops 33554432 | bytes 262144 | tf_op jit(solution)/shard_map/second/pallas_call | solution.py:330
  16.8 0.2 collective-permute-start.6
  17.0 0.2 %second.3.refs_0_ = f32[128,128]{1,0:T(8,128)S(1)} custom-call(f32[128,128]{1,0:T(8,128)S(1)} %second.2.refs_0_, bf16[2,128,128]{2,1,0:T(8,128)(2,1)S(1)} %get-tuple-element.11.refs_0_.refs_1_, bf16[128,128]{1,0:T(8,128)(2,1)S(1)} %collective-permute-done.4.refs_1_.refs_2_, bf16[2,128,128]{2,1,0:T(8,128)(2,1)S(1)} %collective-permute-done.5.refs_2_.refs_3_, ...), custom_call_target="tpu_custom_call" | custom-call | flops 33554432 | bytes 262144 | tf_op jit(solution)/shard_map/second/pallas_call | solution.py:330
  17.2 0.9 %collective-permute-done.6.refs_1_ = f32[128,128]{1,0:T(8,128)S(1)} collective-permute-done((f32[128,128]{1,0:T(8,128)S(1)}, f32[128,128]{1,0:T(8,128)S(1)}, u32[]{:S(2)}, u32[]{:S(2)}) %collective-permute-start.6) | collective-permute-done | bytes 65568 | tf_op jit(solution)/shard_map/ppermute | solution.py:70
  18.1 0.7 %last.1 = f32[128,128]{1,0:T(8,128)} custom-call(f32[128,128]{1,0:T(8,128)S(1)} %second.3.refs_0_, f32[128,128]{1,0:T(8,128)S(1)} %collective-permute-done.6.refs_1_, f32[2,128,128]{2,1,0:T(8,128)S(1)} %restart.1.restart_ref.refs_2_, s32[1,128]{1,0:T(1,128)S(1)} %bitcast.5), custom_call_target="tpu_custom_call" | custom-call | bytes 196608 | tf_op jit(solution)/shard_map/last/pallas_call | solution.py:289
  (2 shorter events, 0.1 us)
Async XLA Ops:
  0.0 6.3 %copy-start = (bf16[1,1,384,128,128]{4,3,2,1,0:T(8,128)(2,1)S(1)}, bf16[1,1,384,128,128]{4,3,2,1,0:T(8,128)(2,1)}, u32[]{:S(2)}) copy-start(bf16[1,1,384,128,128]{4,3,2,1,0:T(8,128)(2,1)} %tiles_ref.1) | copy-start | bytes 37748740
  0.0 6.3 %copy-start.3 = (s32[1,1,384]{2,1,0:T(1,128)S(1)}, s32[1,1,384]{2,1,0:T(1,128)}, u32[]{:S(2)}) copy-start(s32[1,1,384]{2,1,0:T(1,128)} %out_ref.1) | copy-start | bytes 4612
  0.0 6.3 %copy-start.4 = (s32[1,1,384]{2,1,0:T(1,128)S(1)}, s32[1,1,384]{2,1,0:T(1,128)}, u32[]{:S(2)}) copy-start(s32[1,1,384]{2,1,0:T(1,128)} %in_ref.1) | copy-start | bytes 4612
  1.0 8.4 %copy-start.2 = (s32[128]{0:T(128)S(1)}, s32[128]{0:T(128)}, u32[]{:S(2)}) copy-start(s32[128]{0:T(128)} %param.11) | copy-start | bytes 1540
  1.0 8.7 %copy-start.1 = (s32[128,16]{0,1:T(8,128)S(1)}, s32[128,16]{0,1:T(8,128)}, u32[]{:S(2)}) copy-start(s32[128,16]{0,1:T(8,128)} %param.12) | copy-start | bytes 24580
  1.1 6.7 %collective-permute-start.2 = (bf16[128,128]{1,0:T(8,128)(2,1)S(1)}, bf16[128,128]{1,0:T(8,128)(2,1)S(1)}, u32[]{:S(2)}, u32[]{:S(2)}) collective-permute-start(bf16[128,128]{1,0:T(8,128)(2,1)S(1)} %scale.1.after_ref.refs_0_), channel_id=1, source_target_pairs={{12,0},{8,4},{4,8},{0,12},{13,1},{9,5},{5,9},{1,13},{14,2},{10,6},... | collective-permute-start | bytes 98312 | tf_op jit(solution)/shard_map/ppermute | solution.py:52
  5.0 3.9 %collective-permute-start.1 = (bf16[128,128]{1,0:T(8,128)(2,1)S(1)}, bf16[128,128]{1,0:T(8,128)(2,1)S(1)}, u32[]{:S(2)}, u32[]{:S(2)}) collective-permute-start(bf16[128,128]{1,0:T(8,128)(2,1)S(1)} %scale.1.after_ref.refs_0_), channel_id=1, source_target_pairs={{8,0},{12,4},{0,8},{4,12},{9,1},{13,5},{1,9},{5,13},{10,2},{14,6},... | collective-permute-start | bytes 98312 | tf_op jit(solution)/shard_map/ppermute | solution.py:52
  5.5 3.9 %collective-permute-start = (bf16[128,128]{1,0:T(8,128)(2,1)S(1)}, bf16[128,128]{1,0:T(8,128)(2,1)S(1)}, u32[]{:S(2)}, u32[]{:S(2)}) collective-permute-start(bf16[128,128]{1,0:T(8,128)(2,1)S(1)} %scale.1.after_ref.refs_0_), channel_id=1, source_target_pairs={{4,0},{0,4},{12,8},{8,12},{5,1},{1,5},{13,9},{9,13},{6,2},{2,6},{1... | collective-permute-start | bytes 98312 | tf_op jit(solution)/shard_map/ppermute | solution.py:52
  9.7 1.6 %collective-permute-start.3 = (f32[2,264,128]{2,1,0:T(8,128)S(1)}, f32[2,264,128]{2,1,0:T(8,128)S(1)}, u32[]{:S(2)}, u32[]{:S(2)}) collective-permute-start(f32[2,264,128]{2,1,0:T(8,128)S(1)} %first.1.after_ref.mine_ref), channel_id=1, source_target_pairs={{0,16},{16,0},{1,17},{17,1},{2,18},{18,2},{3,19},{19,3},{4,20},{20... | collective-permute-start | bytes 811016 | tf_op jit(solution)/shard_map/ppermute | solution.py:70
  11.3 5.3 %collective-permute-start.5 = (bf16[2,128,128]{2,1,0:T(8,128)(2,1)S(1)}, bf16[2,128,128]{2,1,0:T(8,128)(2,1)S(1)}, u32[]{:S(2)}, u32[]{:S(2)}) collective-permute-start(bf16[2,128,128]{2,1,0:T(8,128)(2,1)S(1)} %get-tuple-element.11.refs_0_.refs_1_), channel_id=1, source_target_pairs={{8,0},{12,4},{0,8},{4,12},{28,16},{24,20},{20,24},{16,28},{9,1},{1... | collective-permute-start | bytes 196616 | tf_op jit(solution)/shard_map/ppermute | solution.py:61
  12.9 3.7 %collective-permute-start.4 = (bf16[128,128]{1,0:T(8,128)(2,1)S(1)}, bf16[128,128]{1,0:T(8,128)(2,1)S(1)}, u32[]{:S(2)}, u32[]{:S(2)}) collective-permute-start(bf16[128,128]{1,0:T(8,128)(2,1)S(1)} %get-tuple-element.12.after_ref), channel_id=1, source_target_pairs={{20,0},{16,4},{28,8},{24,12},{4,16},{0,20},{12,24},{8,28},{21,1},{... | collective-permute-start | bytes 98312 | tf_op jit(solution)/shard_map/ppermute | solution.py:66
  16.8 1.3 %collective-permute-start.6 = (f32[128,128]{1,0:T(8,128)S(1)}, f32[128,128]{1,0:T(8,128)S(1)}, u32[]{:S(2)}, u32[]{:S(2)}) collective-permute-start(f32[128,128]{1,0:T(8,128)S(1)} %second.2.refs_0_), channel_id=1, source_target_pairs={{0,16},{16,0},{1,17},{17,1},{2,18},{18,2},{3,19},{19,3},{4,20},{20... | collective-permute-start | bytes 196616 | tf_op jit(solution)/shard_map/ppermute | solution.py:70

commit v3 on v1

--- a/solution.py
+++ b/solution.py
@@ -21,7 +21,7 @@
 TILES_VMEM = 32 * 1024 * 1024
 SMALL_VMEM = 8 * 1024 * 1024
 STRIPS = 4
-UNROLL = 8
+UNROLL = 32
 DEGREE_LINES = 8
 
 
@@ -57,7 +57,12 @@
 
 
 def from_hop(value, cols):
-    pairs = [(row * cols + (col ^ hop(row)), row * cols + col) for row in range(2) for col in range(cols)]
+    pairs = [((1 - row) * cols + (col ^ hop(row)), row * cols + col) for row in range(2) for col in range(cols)]
+    return lax.ppermute(value, ("row", "col"), pairs)
+
+
+def from_side(value, cols):
+    pairs = [((1 - row) * cols + (col ^ 1), row * cols + col) for row in range(2) for col in range(cols)]
     return lax.ppermute(value, ("row", "col"), pairs)
 
 
@@ -186,7 +191,7 @@
         )
 
 
-def both_kernel(mine_ref, theirs_ref, restart_ref, own_ref, scaled_ref):
+def both_kernel(mine_ref, theirs_ref, restart_ref, other_ref, scaled_ref):
     _, sets, owned = restart_ref.shape
     for place in range(2):
         incoming = mine_ref[place, :sets] + theirs_ref[1 - place, :sets]
@@ -194,8 +199,8 @@
         risk = restart_ref[place] + damping * incoming
         scaled = (risk / degree).astype(jnp.bfloat16)
         scaled_ref[place] = scaled
-        if not place:
-            own_ref[...] = scaled
+        if place:
+            other_ref[...] = scaled
 
 
 def foreign_kernel(after_ref, theirs_ref, weight_ref):
@@ -209,9 +214,9 @@
 
 
 def second_kernel(place, after, *refs):
-    own_ref, side_ref, hop_ref, weight_ref, foreign_ref, result_ref = refs[after:]
+    both_ref, side_ref, hop_ref, weight_ref, foreign_ref, result_ref = refs[after:]
     row, col = lax.axis_index("row"), lax.axis_index("col")
-    parts = [own_ref[...], side_ref[...], hop_ref[0], hop_ref[1]]
+    parts = [both_ref[0], side_ref[...], hop_ref[1], hop_ref[0]]
     weights = [weight_ref[col], weight_ref[col ^ 1], weight_ref[col ^ hop(row)], foreign_ref[place]]
     result_ref[...] = times_weight(parts, weights)
 
@@ -317,7 +322,7 @@
         )(*parts, *weights, degree)
         theirs = swap_rows(mine)
         restart = count_restart(2, mine)
-        own, both = call(
+        other, both = call(
             both_kernel,
             [jax.ShapeDtypeStruct((sets, owned), low), jax.ShapeDtypeStruct((2, sets, owned), low)],
             "both",
@@ -325,7 +330,7 @@
             out_specs=[VMEM] * 2,
             size=24 * sets * owned,
         )(mine, theirs, restart)
-        side = from_column(own, cols, 1)
+        side = from_side(other, cols)
         near = from_hop(both, cols)
         foreign = call(
             foreign_kernel,
@@ -334,7 +339,7 @@
             in_specs=[ANY, VMEM],
             out_specs=VMEM,
             size=16 * owned * owned,
-        )(own, theirs)
+        )(other, theirs)
 
         def second(place, *after):
             return call(
@@ -345,7 +350,7 @@
                 out_specs=VMEM,
                 flops=4 * sets * cols * owned * owned,
                 size=4 * cols * owned * owned,
-            )(*after, own, side, near, weights[place], foreign)
+            )(*after, both, side, near, weights[place], foreign)
 
         leaving = second(1)
         received = swap_rows(leaving)

time: 19.2 us -> 19.1 us (level); the launches traced: 19.1 us -> 19.3 us
  starting transfers between devices: 6.86 us -> 7.45 us
  waiting for transfers between devices: 7.73 us -> 7.41 us
    ppermute x4 -> x3, waiting for transfers between devices: 5.46 us -> 2.14 us  [from_column(): lax.ppermute(value, 'col', [(partner(col, offset, cols), col) for col in...]
    ppermute x0 -> x1, waiting for transfers between devices: none -> 3.02 us  [from_side(): return lax.ppermute(value, ('row', 'col'), pairs)]
    ppermute x1, starting transfers between devices: 1.58 us -> 2.13 us  [from_hop(): return lax.ppermute(value, ('row', 'col'), pairs)]
    ppermute x0 -> x1, starting transfers between devices: none -> 0.54 us  [from_side(): return lax.ppermute(value, ('row', 'col'), pairs)]
    ppermute x4 -> x3, starting transfers between devices: 5.14 us -> 4.6 us  [from_column(): lax.ppermute(value, 'col', [(partner(col, offset, cols), col) for col in...]
where the time goes in v3:
time: 19.1 us; the launch traced here: 19.3 us
  starting transfers between devices  7.45 us (39%)
  waiting for transfers between devices  7.41 us (39%)
  Pallas kernels  3.66 us (19%)
  between operations  0.73 us (4%)
    ppermute x3, starting transfers between devices, from_column(): lax.ppermute(value, 'col', [(partner(col, offset, cols), col) for col in...  4.6 us
    ppermute x1, waiting for transfers between devices, from_side(): return lax.ppermute(value, ('row', 'col'), pairs)  3.02 us
    ppermute x2, waiting for transfers between devices, swap_rows(): return lax.ppermute(value, 'row', [(0, 1), (1, 0)])  2.25 us
    ppermute x3, waiting for transfers between devices, from_column(): lax.ppermute(value, 'col', [(partner(col, offset, cols), col) for col in...  2.14 us
    ppermute x1, starting transfers between devices, from_hop(): return lax.ppermute(value, ('row', 'col'), pairs)  2.13 us
    pallas_call x1, Pallas kernels, local(): call(scale_kernel, [jax.ShapeDtypeStruct((sets, owned), low), pltpu.SMEM(...  1.07 us
    pallas_call x1, Pallas kernels, local(): call(functools.partial(sum_kernel, rows, cols, owned_blocks), [jax.ShapeD...  0.97 us
    pallas_call x1, Pallas kernels, finish(): call(functools.partial(finish_kernel, last), piece if last else jax.Shape...  0.65 us
  transfers between devices with their start and end apart: 7, of which 5 were waited for; matrix products, arithmetic and copies ran while one was open for 0% of the time, Pallas kernels for 8%

profile of v3, /device:TPU:0, one launch (start us, length us, event | category | flops | bytes accessed | tf_op | source)
XLA Modules:
  0.0 19.3 jit_solution(574701653098131945)
XLA Ops:
  0.0 0.0 copy-start
  0.0 1.1 %scale.1 = (bf16[128,128]{1,0:T(8,128)(2,1)S(1)}, s32[1,1,384]{2,1,0:T(1,128)S(4)}, s32[1,1,384]{2,1,0:T(1,128)S(4)}, s32[16,128]{1,0:T(8,128)S(1)}) custom-call(f32[128,128]{1,0:T(8,128)} %prior_hbm.1, s32[1,128]{1,0:T(1,128)} %bitcast.2, s32[1,1,384]{2,1,0:T(1,128)} %out_hbm.1, s32[1,1,384]{2,1,0:T(1,128)} %in_hbm.1, s32[16,128]{1,0:T(8,128)} %bitcast.5), custom_call_target="tpu_custom_call" | custom-call | flops 12884901888 | bytes 98304 | tf_op jit(solution)/shard_map/scale/pallas_call | solution.py:242
  1.1 0.0 copy-start.1
  1.1 4.0 %collective-permute-start.2 = (bf16[128,128]{1,0:T(8,128)(2,1)S(1)}, bf16[128,128]{1,0:T(8,128)(2,1)S(1)}, u32[]{:S(2)}, u32[]{:S(2)}) collective-permute-start(bf16[128,128]{1,0:T(8,128)(2,1)S(1)} %get-tuple-element.13.after_ref.refs_0_), channel_id=1, source_target_pairs={{12,0},{8,4},{4,8},{0,12},{13,1},{9,5},{5,9},{1,13},{14,2},{10,6},... | collective-permute-start | bytes 98312 | tf_op jit(solution)/shard_map/ppermute | solution.py:52
  5.0 0.5 %collective-permute-start.1 = (bf16[128,128]{1,0:T(8,128)(2,1)S(1)}, bf16[128,128]{1,0:T(8,128)(2,1)S(1)}, u32[]{:S(2)}, u32[]{:S(2)}) collective-permute-start(bf16[128,128]{1,0:T(8,128)(2,1)S(1)} %get-tuple-element.13.after_ref.refs_0_), channel_id=1, source_target_pairs={{8,0},{12,4},{0,8},{4,12},{9,1},{13,5},{1,9},{5,13},{10,2},{14,6},... | collective-permute-start | bytes 98312 | tf_op jit(solution)/shard_map/ppermute | solution.py:52
  5.6 0.1 collective-permute-start
  6.3 0.0 copy-done
  6.4 1.0 %sum_tiles.1 = (bf16[4,128,256]{2,1,0:T(8,128)(2,1)S(1)}, bf16[4,128,256]{2,1,0:T(8,128)(2,1)S(1)}) custom-call(bf16[128,128]{1,0:T(8,128)(2,1)S(1)} %get-tuple-element.13.after_ref.refs_0_, s32[1,1]{1,0:T(1,128)S(6)} %copy.8.count_ref, s32[1,1,384]{2,1,0:T(1,128)S(4)} %get-tuple-element.14.out_ref, s32[1,1,384]{2,1,0:T(1,128)S(4)} %get-tuple-element.15.in_ref, ...), custom_call_target="tpu_custom_call" | custom-call | flops 6291456 | bytes 12582912 | tf_op jit(solution)/shard_map/sum_tiles/pallas_call | solution.py:267
  7.3 0.0 collective-permute-done.2.refs_3_
  7.3 1.6 %collective-permute-done.1.refs_2_ = bf16[128,128]{1,0:T(8,128)(2,1)S(1)} collective-permute-done((bf16[128,128]{1,0:T(8,128)(2,1)S(1)}, bf16[128,128]{1,0:T(8,128)(2,1)S(1)}, u32[]{:S(2)}, u32[]{:S(2)}) %collective-permute-start.1) | collective-permute-done | bytes 32800 | tf_op jit(solution)/shard_map/ppermute | solution.py:52
  9.0 0.5 %collective-permute-done.refs_1_ = bf16[128,128]{1,0:T(8,128)(2,1)S(1)} collective-permute-done((bf16[128,128]{1,0:T(8,128)(2,1)S(1)}, bf16[128,128]{1,0:T(8,128)(2,1)S(1)}, u32[]{:S(2)}, u32[]{:S(2)}) %collective-permute-start) | collective-permute-done | bytes 32800 | tf_op jit(solution)/shard_map/ppermute | solution.py:52
  9.5 0.0 copy-done.1
  9.5 0.2 %first.1.after_ref.mine_ref = f32[2,264,128]{2,1,0:T(8,128)S(1)} custom-call(bf16[128,128]{1,0:T(8,128)(2,1)S(1)} %get-tuple-element.13.after_ref.refs_0_, bf16[128,128]{1,0:T(8,128)(2,1)S(1)} %collective-permute-done.refs_1_, bf16[128,128]{1,0:T(8,128)(2,1)S(1)} %collective-permute-done.1.refs_2_, bf16[128,128]{1,0:T(8,128)(2,1)S(1)} %collective-permute-done.2.refs_3_, ...), custom_call_target="tpu_custom_call" | custom-call | flops 67108864 | bytes 524288 | tf_op jit(solution)/shard_map/first/pallas_call | solution.py:314
  9.7 0.1 collective-permute-start.3
  9.8 0.3 %restart.1.restart_ref.refs_2_ = f32[2,128,128]{2,1,0:T(8,128)S(1)} custom-call(f32[2,264,128]{2,1,0:T(8,128)S(1)} %first.1.after_ref.mine_ref, s32[16,128]{1,0:T(8,128)S(1)} %get-tuple-element.18.seeds_ref), custom_call_target="tpu_custom_call" | custom-call | flops 1048576 | bytes 131072 | tf_op jit(solution)/shard_map/restart/pallas_call | solution.py:293
  10.1 1.2 %collective-permute-done.3.theirs_ref = f32[2,264,128]{2,1,0:T(8,128)S(1)} collective-permute-done((f32[2,264,128]{2,1,0:T(8,128)S(1)}, f32[2,264,128]{2,1,0:T(8,128)S(1)}, u32[]{:S(2)}, u32[]{:S(2)}) %collective-permute-start.3) | collective-permute-done | bytes 270368 | tf_op jit(solution)/shard_map/ppermute | solution.py:70
  11.4 2.1 %collective-permute-start.5 = (bf16[2,128,128]{2,1,0:T(8,128)(2,1)S(1)}, bf16[2,128,128]{2,1,0:T(8,128)(2,1)S(1)}, u32[]{:S(2)}, u32[]{:S(2)}) collective-permute-start(bf16[2,128,128]{2,1,0:T(8,128)(2,1)S(1)} %get-tuple-element.19.refs_0_.refs_1_), channel_id=1, source_target_pairs={{24,0},{28,4},{16,8},{20,12},{12,16},{8,20},{4,24},{0,28},{25,1},{... | collective-permute-start | bytes 196616 | tf_op jit(solution)/shard_map/ppermute | solution.py:61
  13.5 0.5 %collective-permute-start.4 = (bf16[128,128]{1,0:T(8,128)(2,1)S(1)}, bf16[128,128]{1,0:T(8,128)(2,1)S(1)}, u32[]{:S(2)}, u32[]{:S(2)}) collective-permute-start(bf16[128,128]{1,0:T(8,128)(2,1)S(1)} %get-tuple-element.20.after_ref), channel_id=1, source_target_pairs={{20,0},{16,4},{28,8},{24,12},{4,16},{0,20},{12,24},{8,28},{21,1},{... | collective-permute-start | bytes 98312 | tf_op jit(solution)/shard_map/ppermute | solution.py:66
  14.1 3.0 %collective-permute-done.4.refs_1_.refs_2_ = bf16[128,128]{1,0:T(8,128)(2,1)S(1)} collective-permute-done((bf16[128,128]{1,0:T(8,128)(2,1)S(1)}, bf16[128,128]{1,0:T(8,128)(2,1)S(1)}, u32[]{:S(2)}, u32[]{:S(2)}) %collective-permute-start.4) | collective-permute-done | bytes 32800 | tf_op jit(solution)/shard_map/ppermute | solution.py:66
  17.1 0.0 collective-permute-done.5.refs_2_.refs_3_
  17.1 0.2 %second.2.refs_0_ = f32[128,128]{1,0:T(8,128)S(1)} custom-call(bf16[2,128,128]{2,1,0:T(8,128)(2,1)S(1)} %get-tuple-element.19.refs_0_.refs_1_, bf16[128,128]{1,0:T(8,128)(2,1)S(1)} %collective-permute-done.4.refs_1_.refs_2_, bf16[2,128,128]{2,1,0:T(8,128)(2,1)S(1)} %collective-permute-done.5.refs_2_.refs_3_, ...), custom_call_target="tpu_custom_call" | custom-call | flops 33554432 | bytes 262144 | tf_op jit(solution)/shard_map/second/pallas_call | solution.py:345
  17.3 0.1 collective-permute-start.6
  17.4 0.2 second.3.refs_0_
  17.6 1.0 %collective-permute-done.6.refs_1_ = f32[128,128]{1,0:T(8,128)S(1)} collective-permute-done((f32[128,128]{1,0:T(8,128)S(1)}, f32[128,128]{1,0:T(8,128)S(1)}, u32[]{:S(2)}, u32[]{:S(2)}) %collective-permute-start.6) | collective-permute-done | bytes 65568 | tf_op jit(solution)/shard_map/ppermute | solution.py:70
  18.6 0.7 %last.1 = f32[128,128]{1,0:T(8,128)} custom-call(f32[128,128]{1,0:T(8,128)S(1)} %second.3.refs_0_, f32[128,128]{1,0:T(8,128)S(1)} %collective-permute-done.6.refs_1_, f32[2,128,128]{2,1,0:T(8,128)S(1)} %restart.1.restart_ref.refs_2_, s32[1,128]{1,0:T(1,128)S(1)} %bitcast.4), custom_call_target="tpu_custom_call" | custom-call | bytes 196608 | tf_op jit(solution)/shard_map/last/pallas_call | solution.py:304
  (2 shorter events, 0.1 us)
Async XLA Ops:
  0.0 6.3 %copy-start = (bf16[1,1,384,128,128]{4,3,2,1,0:T(8,128)(2,1)S(1)}, bf16[1,1,384,128,128]{4,3,2,1,0:T(8,128)(2,1)}, u32[]{:S(2)}) copy-start(bf16[1,1,384,128,128]{4,3,2,1,0:T(8,128)(2,1)} %tiles_ref.1) | copy-start | bytes 37748740
  1.1 8.4 %copy-start.1 = (s32[128]{0:T(128)S(1)}, s32[128]{0:T(128)}, u32[]{:S(2)}) copy-start(s32[128]{0:T(128)} %param.11) | copy-start | bytes 1540
  1.1 6.2 %collective-permute-start.2 = (bf16[128,128]{1,0:T(8,128)(2,1)S(1)}, bf16[128,128]{1,0:T(8,128)(2,1)S(1)}, u32[]{:S(2)}, u32[]{:S(2)}) collective-permute-start(bf16[128,128]{1,0:T(8,128)(2,1)S(1)} %get-tuple-element.13.after_ref.refs_0_), channel_id=1, source_target_pairs={{12,0},{8,4},{4,8},{0,12},{13,1},{9,5},{5,9},{1,13},{14,2},{10,6},... | collective-permute-start | bytes 98312 | tf_op jit(solution)/shard_map/ppermute | solution.py:52
  5.0 3.9 %collective-permute-start.1 = (bf16[128,128]{1,0:T(8,128)(2,1)S(1)}, bf16[128,128]{1,0:T(8,128)(2,1)S(1)}, u32[]{:S(2)}, u32[]{:S(2)}) collective-permute-start(bf16[128,128]{1,0:T(8,128)(2,1)S(1)} %get-tuple-element.13.after_ref.refs_0_), channel_id=1, source_target_pairs={{8,0},{12,4},{0,8},{4,12},{9,1},{13,5},{1,9},{5,13},{10,2},{14,6},... | collective-permute-start | bytes 98312 | tf_op jit(solution)/shard_map/ppermute | solution.py:52
  5.6 3.9 %collective-permute-start = (bf16[128,128]{1,0:T(8,128)(2,1)S(1)}, bf16[128,128]{1,0:T(8,128)(2,1)S(1)}, u32[]{:S(2)}, u32[]{:S(2)}) collective-permute-start(bf16[128,128]{1,0:T(8,128)(2,1)S(1)} %get-tuple-element.13.after_ref.refs_0_), channel_id=1, source_target_pairs={{4,0},{0,4},{12,8},{8,12},{5,1},{1,5},{13,9},{9,13},{6,2},{2,6},{1... | collective-permute-start | bytes 98312 | tf_op jit(solution)/shard_map/ppermute | solution.py:52
  9.7 1.6 %collective-permute-start.3 = (f32[2,264,128]{2,1,0:T(8,128)S(1)}, f32[2,264,128]{2,1,0:T(8,128)S(1)}, u32[]{:S(2)}, u32[]{:S(2)}) collective-permute-start(f32[2,264,128]{2,1,0:T(8,128)S(1)} %first.1.after_ref.mine_ref), channel_id=1, source_target_pairs={{0,16},{16,0},{1,17},{17,1},{2,18},{18,2},{3,19},{19,3},{4,20},{20... | collective-permute-start | bytes 811016 | tf_op jit(solution)/shard_map/ppermute | solution.py:70
  11.4 5.7 %collective-permute-start.5 = (bf16[2,128,128]{2,1,0:T(8,128)(2,1)S(1)}, bf16[2,128,128]{2,1,0:T(8,128)(2,1)S(1)}, u32[]{:S(2)}, u32[]{:S(2)}) collective-permute-start(bf16[2,128,128]{2,1,0:T(8,128)(2,1)S(1)} %get-tuple-element.19.refs_0_.refs_1_), channel_id=1, source_target_pairs={{24,0},{28,4},{16,8},{20,12},{12,16},{8,20},{4,24},{0,28},{25,1},{... | collective-permute-start | bytes 196616 | tf_op jit(solution)/shard_map/ppermute | solution.py:61
  13.5 3.6 %collective-permute-start.4 = (bf16[128,128]{1,0:T(8,128)(2,1)S(1)}, bf16[128,128]{1,0:T(8,128)(2,1)S(1)}, u32[]{:S(2)}, u32[]{:S(2)}) collective-permute-start(bf16[128,128]{1,0:T(8,128)(2,1)S(1)} %get-tuple-element.20.after_ref), channel_id=1, source_target_pairs={{20,0},{16,4},{28,8},{24,12},{4,16},{0,20},{12,24},{8,28},{21,1},{... | collective-permute-start | bytes 98312 | tf_op jit(solution)/shard_map/ppermute | solution.py:66
  17.3 1.3 %collective-permute-start.6 = (f32[128,128]{1,0:T(8,128)S(1)}, f32[128,128]{1,0:T(8,128)S(1)}, u32[]{:S(2)}, u32[]{:S(2)}) collective-permute-start(f32[128,128]{1,0:T(8,128)S(1)} %second.2.refs_0_), channel_id=1, source_target_pairs={{0,16},{16,0},{1,17},{17,1},{2,18},{18,2},{3,19},{19,3},{4,20},{20... | collective-permute-start | bytes 196616 | tf_op jit(solution)/shard_map/ppermute | solution.py:70

commit v4 on v3

--- a/solution.py
+++ b/solution.py
@@ -175,11 +175,11 @@
 
 
 def first_kernel(cols, *refs):
-    part_refs, (own_ref, other_ref, degree_ref, given_ref) = refs[:cols], refs[cols:]
+    part_refs, (own_ref, other_ref, degree_ref, given_ref) = refs[:cols - 1], refs[cols - 1:]
     row, col = lax.axis_index("row"), lax.axis_index("col")
     parts = [ref[...] for ref in part_refs]
     sets, owned = parts[0].shape
-    columns = [partner(col, offset, cols) for offset in range(cols)]
+    columns = [col] + [partner(col, offset, cols) for offset in range(2, cols)]
     wanted = col ^ hop(1 - row)
     for place, weight_ref in enumerate((own_ref, other_ref)):
         given_ref[place, :sets] = times_weight(parts, [weight_ref[column] for column in columns])
@@ -189,6 +189,14 @@
         given_ref[place, sets + owned:] = jnp.broadcast_to(
             degree_ref[...].astype(jnp.float32), (given_ref.shape[1] - sets - owned, owned)
         )
+
+
+def nearest_kernel(early_ref, part_ref, own_ref, other_ref, given_ref):
+    col = lax.axis_index("col")
+    sets = part_ref.shape[0]
+    for place, weight_ref in enumerate((own_ref, other_ref)):
+        given_ref[place, :sets] = early_ref[place, :sets] + times_weight([part_ref[...]], [weight_ref[col ^ 1]])
+        given_ref[place, sets:] = early_ref[place, sets:]
 
 
 def both_kernel(mine_ref, theirs_ref, restart_ref, other_ref, scaled_ref):
@@ -214,11 +222,15 @@
 
 
 def second_kernel(place, after, *refs):
-    both_ref, side_ref, hop_ref, weight_ref, foreign_ref, result_ref = refs[after:]
+    both_ref, hop_ref, weight_ref, foreign_ref, result_ref = refs[after:]
     row, col = lax.axis_index("row"), lax.axis_index("col")
-    parts = [both_ref[0], side_ref[...], hop_ref[1], hop_ref[0]]
-    weights = [weight_ref[col], weight_ref[col ^ 1], weight_ref[col ^ hop(row)], foreign_ref[place]]
+    parts = [hop_ref[1], hop_ref[0], both_ref[0]]
+    weights = [weight_ref[col ^ hop(row)], foreign_ref[place], weight_ref[col]]
     result_ref[...] = times_weight(parts, weights)
+
+
+def side_kernel(early_ref, side_ref, weight_ref, result_ref):
+    result_ref[...] = early_ref[...] + times_weight([side_ref[...]], [weight_ref[lax.axis_index("col") ^ 1]])
 
 
 def finish_kernel(last, *refs):
@@ -311,15 +323,25 @@
         )(*incoming, restart, degree)
 
     if (rows, cols, ITERATIONS) == (2, 4, 2):
+        given = jax.ShapeDtypeStruct((2, sets + owned + DEGREE_LINES, owned), jnp.float32)
+        early = call(
+            functools.partial(first_kernel, cols),
+            given,
+            "first",
+            in_specs=[VMEM] * (cols + 2),
+            out_specs=VMEM,
+            flops=8 * sets * (cols - 1) * owned * owned,
+            size=8 * cols * owned * owned,
+        )(parts[0], *parts[2:], *weights, degree)
         mine = call(
-            functools.partial(first_kernel, cols),
-            jax.ShapeDtypeStruct((2, sets + owned + DEGREE_LINES, owned), jnp.float32),
-            "first",
-            in_specs=[VMEM] * (cols + 3),
+            nearest_kernel,
+            given,
+            "nearest",
+            in_specs=[VMEM] * 4,
             out_specs=VMEM,
-            flops=8 * sets * cols * owned * owned,
-            size=8 * cols * owned * owned,
-        )(*parts, *weights, degree)
+            flops=8 * sets * owned * owned,
+            size=24 * sets * owned,
+        )(early, parts[1], *weights)
         theirs = swap_rows(mine)
         restart = count_restart(2, mine)
         other, both = call(
@@ -342,15 +364,24 @@
         )(other, theirs)
 
         def second(place, *after):
-            return call(
+            early = call(
                 functools.partial(second_kernel, place, len(after)),
                 piece,
                 "second",
-                in_specs=[ANY] * len(after) + [VMEM] * 5,
+                in_specs=[ANY] * len(after) + [VMEM] * 4,
                 out_specs=VMEM,
-                flops=4 * sets * cols * owned * owned,
-                size=4 * cols * owned * owned,
-            )(*after, both, side, near, weights[place], foreign)
+                flops=12 * sets * owned * owned,
+                size=12 * owned * owned,
+            )(*after, both, near, weights[place], foreign)
+            return call(
+                side_kernel,
+                piece,
+                "side",
+                in_specs=[VMEM] * 3,
+                out_specs=VMEM,
+                flops=4 * sets * owned * owned,
+                size=16 * sets * owned,
+            )(early, side, weights[place])
 
         leaving = second(1)
         received = swap_rows(leaving)

time: 19.1 us -> 19.1 us (level)
  waiting for transfers between devices: 7.41 us -> 5.17 us
  Pallas kernels: 3.66 us -> 5.71 us
    ppermute x3, waiting for transfers between devices: 2.14 us -> 0.3 us  [from_column(): lax.ppermute(value, 'col', [(partner(col, offset, cols), col) for col in...]
    ppermute x1, waiting for transfers between devices: 3.02 us -> 1.19 us  [from_side(): return lax.ppermute(value, ('row', 'col'), pairs)]
    pallas_call x1, Pallas kernels: 0.97 us -> 2.57 us  [local(): call(functools.partial(sum_kernel, rows, cols, owned_blocks), [jax.ShapeD...]
    ppermute x1, waiting for transfers between devices: 0.01 us -> 1.57 us  [from_hop(): return lax.ppermute(value, ('row', 'col'), pairs)]
    pallas_call x1 -> x4, Pallas kernels: 0.24 us -> 0.71 us  [the longest x2 0.3 us: second(): call(side_kernel, piece, 'side', in_specs=[VMEM] * 3, out_specs=VMEM, flo...]
    ppermute x1, starting transfers between devices: 2.13 us -> 2.35 us  [from_hop(): return lax.ppermute(value, ('row', 'col'), pairs)]
  transfers between devices with their start and end apart: 7 -> 7, of which waited for: 5 -> 5; matrix products, arithmetic and copies ran while one was open for 0% -> 0% of each run, Pallas kernels for 8% -> 19%
where the time goes in v4:
time: 19.1 us; the launch traced here: 19.3 us
  starting transfers between devices  7.64 us (40%)
  Pallas kernels  5.71 us (30%)
  waiting for transfers between devices  5.17 us (27%)
  between operations  0.76 us (4%)
    ppermute x3, starting transfers between devices, from_column(): lax.ppermute(value, 'col', [(partner(col, offset, cols), col) for col in...  4.6 us
    pallas_call x1, Pallas kernels, local(): call(functools.partial(sum_kernel, rows, cols, owned_blocks), [jax.ShapeD...  2.57 us
    ppermute x1, starting transfers between devices, from_hop(): return lax.ppermute(value, ('row', 'col'), pairs)  2.35 us
    ppermute x2, waiting for transfers between devices, swap_rows(): return lax.ppermute(value, 'row', [(0, 1), (1, 0)])  2.12 us
    ppermute x1, waiting for transfers between devices, from_hop(): return lax.ppermute(value, ('row', 'col'), pairs)  1.57 us
    ppermute x1, waiting for transfers between devices, from_side(): return lax.ppermute(value, ('row', 'col'), pairs)  1.19 us
    pallas_call x1, Pallas kernels, local(): call(scale_kernel, [jax.ShapeDtypeStruct((sets, owned), low), pltpu.SMEM(...  1.07 us
    pallas_call x1, Pallas kernels, finish(): call(functools.partial(finish_kernel, last), piece if last else jax.Shape...  0.64 us
  transfers between devices with their start and end apart: 7, of which 5 were waited for; matrix products, arithmetic and copies ran while one was open for 0% of the time, Pallas kernels for 19%

profile of v4, /device:TPU:0, one launch (start us, length us, event | category | flops | bytes accessed | tf_op | source)
XLA Modules:
  0.0 19.3 jit_solution(4105165664724747914)
XLA Ops:
  0.0 0.0 copy-start
  0.0 1.1 %scale.1 = (bf16[128,128]{1,0:T(8,128)(2,1)S(1)}, s32[1,1,384]{2,1,0:T(1,128)S(4)}, s32[1,1,384]{2,1,0:T(1,128)S(4)}, s32[16,128]{1,0:T(8,128)S(1)}) custom-call(f32[128,128]{1,0:T(8,128)} %prior_hbm.1, s32[1,128]{1,0:T(1,128)} %bitcast.2, s32[1,1,384]{2,1,0:T(1,128)} %out_hbm.1, s32[1,1,384]{2,1,0:T(1,128)} %in_hbm.1, s32[16,128]{1,0:T(8,128)} %bitcast.5), custom_call_target="tpu_custom_call" | custom-call | flops 12884901888 | bytes 98304 | tf_op jit(solution)/shard_map/scale/pallas_call | solution.py:254
  1.1 0.0 copy-start.1
  1.1 4.0 %collective-permute-start.1 = (bf16[128,128]{1,0:T(8,128)(2,1)S(1)}, bf16[128,128]{1,0:T(8,128)(2,1)S(1)}, u32[]{:S(2)}, u32[]{:S(2)}) collective-permute-start(bf16[128,128]{1,0:T(8,128)(2,1)S(1)} %get-tuple-element.13.after_ref.refs_0_), channel_id=1, source_target_pairs={{12,0},{8,4},{4,8},{0,12},{13,1},{9,5},{5,9},{1,13},{14,2},{10,6},... | collective-permute-start | bytes 98312 | tf_op jit(solution)/shard_map/ppermute | solution.py:52
  5.0 0.5 %collective-permute-start = (bf16[128,128]{1,0:T(8,128)(2,1)S(1)}, bf16[128,128]{1,0:T(8,128)(2,1)S(1)}, u32[]{:S(2)}, u32[]{:S(2)}) collective-permute-start(bf16[128,128]{1,0:T(8,128)(2,1)S(1)} %get-tuple-element.13.after_ref.refs_0_), channel_id=1, source_target_pairs={{8,0},{12,4},{0,8},{4,12},{9,1},{13,5},{1,9},{5,13},{10,2},{14,6},... | collective-permute-start | bytes 98312 | tf_op jit(solution)/shard_map/ppermute | solution.py:52
  5.6 0.1 collective-permute-start.2
  6.3 0.0 copy-done
  6.4 2.6 %sum_tiles.1 = (bf16[4,128,256]{2,1,0:T(8,128)(2,1)S(1)}, bf16[4,128,256]{2,1,0:T(8,128)(2,1)S(1)}) custom-call(bf16[128,128]{1,0:T(8,128)(2,1)S(1)} %get-tuple-element.13.after_ref.refs_0_, s32[1,1]{1,0:T(1,128)S(6)} %copy.8.count_ref, s32[1,1,384]{2,1,0:T(1,128)S(4)} %get-tuple-element.14.out_ref, s32[1,1,384]{2,1,0:T(1,128)S(4)} %get-tuple-element.15.in_ref, ...), custom_call_target="tpu_custom_call" | custom-call | flops 6291456 | bytes 12582912 | tf_op jit(solution)/shard_map/sum_tiles/pallas_call | solution.py:279
  8.9 0.0 collective-permute-done.1.refs_2_
  8.9 0.0 collective-permute-done.refs_1_
  9.0 0.0 copy-done.1
  9.0 0.2 %first.1.early_ref = f32[2,264,128]{2,1,0:T(8,128)S(1)} custom-call(bf16[128,128]{1,0:T(8,128)(2,1)S(1)} %get-tuple-element.13.after_ref.refs_0_, bf16[128,128]{1,0:T(8,128)(2,1)S(1)} %collective-permute-done.refs_1_, bf16[128,128]{1,0:T(8,128)(2,1)S(1)} %collective-permute-done.1.refs_2_, ...), custom_call_target="tpu_custom_call" | custom-call | flops 50331648 | bytes 524288 | tf_op jit(solution)/shard_map/first/pallas_call | solution.py:327
  9.2 0.3 %collective-permute-done.2.part_ref = bf16[128,128]{1,0:T(8,128)(2,1)S(1)} collective-permute-done((bf16[128,128]{1,0:T(8,128)(2,1)S(1)}, bf16[128,128]{1,0:T(8,128)(2,1)S(1)}, u32[]{:S(2)}, u32[]{:S(2)}) %collective-permute-start.2) | collective-permute-done | bytes 32800 | tf_op jit(solution)/shard_map/ppermute | solution.py:52
  9.5 0.2 nearest.1.after_ref.mine_ref
  9.7 0.1 collective-permute-start.3
  9.7 0.3 %restart.1.restart_ref.refs_2_ = f32[2,128,128]{2,1,0:T(8,128)S(1)} custom-call(f32[2,264,128]{2,1,0:T(8,128)S(1)} %nearest.1.after_ref.mine_ref, s32[16,128]{1,0:T(8,128)S(1)} %get-tuple-element.18.seeds_ref), custom_call_target="tpu_custom_call" | custom-call | flops 1048576 | bytes 131072 | tf_op jit(solution)/shard_map/restart/pallas_call | solution.py:305
  10.0 1.2 %collective-permute-done.3.theirs_ref = f32[2,264,128]{2,1,0:T(8,128)S(1)} collective-permute-done((f32[2,264,128]{2,1,0:T(8,128)S(1)}, f32[2,264,128]{2,1,0:T(8,128)S(1)}, u32[]{:S(2)}, u32[]{:S(2)}) %collective-permute-start.3) | collective-permute-done | bytes 270368 | tf_op jit(solution)/shard_map/ppermute | solution.py:70
  11.3 2.3 %collective-permute-start.4 = (bf16[2,128,128]{2,1,0:T(8,128)(2,1)S(1)}, bf16[2,128,128]{2,1,0:T(8,128)(2,1)S(1)}, u32[]{:S(2)}, u32[]{:S(2)}) collective-permute-start(bf16[2,128,128]{2,1,0:T(8,128)(2,1)S(1)} %get-tuple-element.19.refs_0_.refs_1_), channel_id=1, source_target_pairs={{24,0},{28,4},{16,8},{20,12},{12,16},{8,20},{4,24},{0,28},{25,1},{... | collective-permute-start | bytes 196616 | tf_op jit(solution)/shard_map/ppermute | solution.py:61
  13.7 0.5 %collective-permute-start.5 = (bf16[128,128]{1,0:T(8,128)(2,1)S(1)}, bf16[128,128]{1,0:T(8,128)(2,1)S(1)}, u32[]{:S(2)}, u32[]{:S(2)}) collective-permute-start(bf16[128,128]{1,0:T(8,128)(2,1)S(1)} %get-tuple-element.20.after_ref), channel_id=1, source_target_pairs={{20,0},{16,4},{28,8},{24,12},{4,16},{0,20},{12,24},{8,28},{21,1},{... | collective-permute-start | bytes 98312 | tf_op jit(solution)/shard_map/ppermute | solution.py:66
  14.2 1.6 %collective-permute-done.4.refs_1_.refs_2_ = bf16[2,128,128]{2,1,0:T(8,128)(2,1)S(1)} collective-permute-done((bf16[2,128,128]{2,1,0:T(8,128)(2,1)S(1)}, bf16[2,128,128]{2,1,0:T(8,128)(2,1)S(1)}, u32[]{:S(2)}, u32[]{:S(2)}) %collective-permute-start.4) | collective-permute-done | bytes 65568 | tf_op jit(solution)/shard_map/ppermute | solution.py:61
  15.8 0.2 second.2.early_ref
  16.0 1.2 %collective-permute-done.5.side_ref = bf16[128,128]{1,0:T(8,128)(2,1)S(1)} collective-permute-done((bf16[128,128]{1,0:T(8,128)(2,1)S(1)}, bf16[128,128]{1,0:T(8,128)(2,1)S(1)}, u32[]{:S(2)}, u32[]{:S(2)}) %collective-permute-start.5) | collective-permute-done | bytes 32800 | tf_op jit(solution)/shard_map/ppermute | solution.py:66
  17.2 0.1 side.2.refs_0_
  17.3 0.1 collective-permute-start.6
  17.4 0.2 second.3.early_ref
  17.6 0.2 side.3.refs_0_
  17.8 0.9 %collective-permute-done.6.refs_1_ = f32[128,128]{1,0:T(8,128)S(1)} collective-permute-done((f32[128,128]{1,0:T(8,128)S(1)}, f32[128,128]{1,0:T(8,128)S(1)}, u32[]{:S(2)}, u32[]{:S(2)}) %collective-permute-start.6) | collective-permute-done | bytes 65568 | tf_op jit(solution)/shard_map/ppermute | solution.py:70
  18.6 0.6 %last.1 = f32[128,128]{1,0:T(8,128)} custom-call(f32[128,128]{1,0:T(8,128)S(1)} %side.3.refs_0_, f32[128,128]{1,0:T(8,128)S(1)} %collective-permute-done.6.refs_1_, f32[2,128,128]{2,1,0:T(8,128)S(1)} %restart.1.restart_ref.refs_2_, s32[1,128]{1,0:T(1,128)S(1)} %bitcast.4), custom_call_target="tpu_custom_call" | custom-call | bytes 196608 | tf_op jit(solution)/shard_map/last/pallas_call | solution.py:316
  (2 shorter events, 0.1 us)
Async XLA Ops:
  0.0 6.3 %copy-start = (bf16[1,1,384,128,128]{4,3,2,1,0:T(8,128)(2,1)S(1)}, bf16[1,1,384,128,128]{4,3,2,1,0:T(8,128)(2,1)}, u32[]{:S(2)}) copy-start(bf16[1,1,384,128,128]{4,3,2,1,0:T(8,128)(2,1)} %tiles_ref.1) | copy-start | bytes 37748740
  1.1 7.9 %copy-start.1 = (s32[128]{0:T(128)S(1)}, s32[128]{0:T(128)}, u32[]{:S(2)}) copy-start(s32[128]{0:T(128)} %param.11) | copy-start | bytes 1540
  1.1 7.8 %collective-permute-start.1 = (bf16[128,128]{1,0:T(8,128)(2,1)S(1)}, bf16[128,128]{1,0:T(8,128)(2,1)S(1)}, u32[]{:S(2)}, u32[]{:S(2)}) collective-permute-start(bf16[128,128]{1,0:T(8,128)(2,1)S(1)} %get-tuple-element.13.after_ref.refs_0_), channel_id=1, source_target_pairs={{12,0},{8,4},{4,8},{0,12},{13,1},{9,5},{5,9},{1,13},{14,2},{10,6},... | collective-permute-start | bytes 98312 | tf_op jit(solution)/shard_map/ppermute | solution.py:52
  5.0 3.9 %collective-permute-start = (bf16[128,128]{1,0:T(8,128)(2,1)S(1)}, bf16[128,128]{1,0:T(8,128)(2,1)S(1)}, u32[]{:S(2)}, u32[]{:S(2)}) collective-permute-start(bf16[128,128]{1,0:T(8,128)(2,1)S(1)} %get-tuple-element.13.after_ref.refs_0_), channel_id=1, source_target_pairs={{8,0},{12,4},{0,8},{4,12},{9,1},{13,5},{1,9},{5,13},{10,2},{14,6},... | collective-permute-start | bytes 98312 | tf_op jit(solution)/shard_map/ppermute | solution.py:52
  5.6 3.9 %collective-permute-start.2 = (bf16[128,128]{1,0:T(8,128)(2,1)S(1)}, bf16[128,128]{1,0:T(8,128)(2,1)S(1)}, u32[]{:S(2)}, u32[]{:S(2)}) collective-permute-start(bf16[128,128]{1,0:T(8,128)(2,1)S(1)} %get-tuple-element.13.after_ref.refs_0_), channel_id=1, source_target_pairs={{4,0},{0,4},{12,8},{8,12},{5,1},{1,5},{13,9},{9,13},{6,2},{2,6},{1... | collective-permute-start | bytes 98312 | tf_op jit(solution)/shard_map/ppermute | solution.py:52
  9.7 1.6 %collective-permute-start.3 = (f32[2,264,128]{2,1,0:T(8,128)S(1)}, f32[2,264,128]{2,1,0:T(8,128)S(1)}, u32[]{:S(2)}, u32[]{:S(2)}) collective-permute-start(f32[2,264,128]{2,1,0:T(8,128)S(1)} %nearest.1.after_ref.mine_ref), channel_id=1, source_target_pairs={{0,16},{16,0},{1,17},{17,1},{2,18},{18,2},{3,19},{19,3},{4,20},{20... | collective-permute-start | bytes 811016 | tf_op jit(solution)/shard_map/ppermute | solution.py:70
  11.3 4.5 %collective-permute-start.4 = (bf16[2,128,128]{2,1,0:T(8,128)(2,1)S(1)}, bf16[2,128,128]{2,1,0:T(8,128)(2,1)S(1)}, u32[]{:S(2)}, u32[]{:S(2)}) collective-permute-start(bf16[2,128,128]{2,1,0:T(8,128)(2,1)S(1)} %get-tuple-element.19.refs_0_.refs_1_), channel_id=1, source_target_pairs={{24,0},{28,4},{16,8},{20,12},{12,16},{8,20},{4,24},{0,28},{25,1},{... | collective-permute-start | bytes 196616 | tf_op jit(solution)/shard_map/ppermute | solution.py:61
  13.7 3.5 %collective-permute-start.5 = (bf16[128,128]{1,0:T(8,128)(2,1)S(1)}, bf16[128,128]{1,0:T(8,128)(2,1)S(1)}, u32[]{:S(2)}, u32[]{:S(2)}) collective-permute-start(bf16[128,128]{1,0:T(8,128)(2,1)S(1)} %get-tuple-element.20.after_ref), channel_id=1, source_target_pairs={{20,0},{16,4},{28,8},{24,12},{4,16},{0,20},{12,24},{8,28},{21,1},{... | collective-permute-start | bytes 98312 | tf_op jit(solution)/shard_map/ppermute | solution.py:66
  17.3 1.3 %collective-permute-start.6 = (f32[128,128]{1,0:T(8,128)S(1)}, f32[128,128]{1,0:T(8,128)S(1)}, u32[]{:S(2)}, u32[]{:S(2)}) collective-permute-start(f32[128,128]{1,0:T(8,128)S(1)} %side.2.refs_0_), channel_id=1, source_target_pairs={{0,16},{16,0},{1,17},{17,1},{2,18},{18,2},{3,19},{19,3},{4,20},{20... | collective-permute-start | bytes 196616 | tf_op jit(solution)/shard_map/ppermute | solution.py:70

commit v5 on v4

--- a/solution.py
+++ b/solution.py
@@ -22,6 +22,7 @@
 SMALL_VMEM = 8 * 1024 * 1024
 STRIPS = 4
 UNROLL = 32
+PIECES = 4
 DEGREE_LINES = 8
 
 
@@ -74,21 +75,23 @@
     prior_hbm, degree_hbm, out_hbm, in_hbm, seeds_hbm,
     scaled_ref, out_ref, in_ref, seeds_ref, prior_ref, degree_ref, arrived,
 ):
-    moves = (
-        (prior_hbm, prior_ref), (degree_hbm, degree_ref),
-        (out_hbm, out_ref), (in_hbm, in_ref), (seeds_hbm, seeds_ref),
-    )
+    pieces = prior_ref.shape[0] // PIECES
+    moves = [(degree_hbm, degree_ref)]
+    for piece in range(PIECES):
+        lines = pl.ds(piece * pieces, pieces)
+        moves.append((prior_hbm.at[lines], prior_ref.at[lines]))
+    moves += [(out_hbm, out_ref), (in_hbm, in_ref), (seeds_hbm, seeds_ref)]
     copies = [
         pltpu.make_async_copy(source, place, arrived.at[index])
         for index, (source, place) in enumerate(moves)
     ]
     for copy in copies:
         copy.start()
-    for copy in copies[:2]:
+    for copy in copies[:1 + PIECES]:
         copy.wait()
     scaled = (prior_ref[...] / degree_ref[...].astype(jnp.float32)).astype(jnp.bfloat16)
     scaled_ref[...] = scaled
-    for copy in copies[2:]:
+    for copy in copies[1 + PIECES:]:
         copy.wait()
 
 
@@ -265,7 +268,7 @@
         scratch_shapes=[
             pltpu.VMEM((sets, owned), jnp.float32),
             pltpu.VMEM((1, owned), jnp.int32),
-            pltpu.SemaphoreType.DMA((5,)),
+            pltpu.SemaphoreType.DMA((4 + PIECES,)),
         ],
         flops=16 * slots * edge**3,
         size=6 * sets * owned,

time: 19.1 us -> 18.7 us (0.979); the launches traced: 19.3 us -> 18.5 us
  waiting for transfers between devices: 5.17 us -> 4.8 us
  starting transfers between devices: 7.64 us -> 7.28 us
    ppermute x1, starting transfers between devices: 2.35 us -> 1.28 us  [from_hop(): return lax.ppermute(value, ('row', 'col'), pairs)]
    ppermute x2, starting transfers between devices: 0.14 us -> 0.85 us  [swap_rows(): return lax.ppermute(value, 'row', [(0, 1), (1, 0)])]
    ppermute x1, waiting for transfers between devices: 1.19 us -> 0.85 us  [from_side(): return lax.ppermute(value, ('row', 'col'), pairs)]
    ppermute x2, waiting for transfers between devices: 2.12 us -> 1.79 us  [swap_rows(): return lax.ppermute(value, 'row', [(0, 1), (1, 0)])]
    ppermute x1, waiting for transfers between devices: 1.57 us -> 1.89 us  [from_hop(): return lax.ppermute(value, ('row', 'col'), pairs)]
  transfers between devices with their start and end apart: 7 -> 7, of which waited for: 5 -> 5; matrix products, arithmetic and copies ran while one was open for 0% -> 0% of each run, Pallas kernels for 19% -> 20%
where the time goes in v5:
time: 18.7 us; the launch traced here: 18.5 us
  starting transfers between devices  7.28 us (39%)
  Pallas kernels  5.69 us (30%)
  waiting for transfers between devices  4.8 us (26%)
  between operations  0.75 us (4%)
    ppermute x3, starting transfers between devices, from_column(): lax.ppermute(value, 'col', [(partner(col, offset, cols), col) for col in...  4.6 us
    pallas_call x1, Pallas kernels, local(): call(functools.partial(sum_kernel, rows, cols, owned_blocks), [jax.ShapeD...  2.58 us
    ppermute x1, waiting for transfers between devices, from_hop(): return lax.ppermute(value, ('row', 'col'), pairs)  1.89 us
    ppermute x2, waiting for transfers between devices, swap_rows(): return lax.ppermute(value, 'row', [(0, 1), (1, 0)])  1.79 us
    ppermute x1, starting transfers between devices, from_hop(): return lax.ppermute(value, ('row', 'col'), pairs)  1.28 us
    pallas_call x1, Pallas kernels, local(): call(scale_kernel, [jax.ShapeDtypeStruct((sets, owned), low), pltpu.SMEM(...  1.03 us
    ppermute x2, starting transfers between devices, swap_rows(): return lax.ppermute(value, 'row', [(0, 1), (1, 0)])  0.85 us
    ppermute x1, waiting for transfers between devices, from_side(): return lax.ppermute(value, ('row', 'col'), pairs)  0.85 us
  transfers between devices with their start and end apart: 7, of which 5 were waited for; matrix products, arithmetic and copies ran while one was open for 0% of the time, Pallas kernels for 20%

profile of v5, /device:TPU:0, one launch (start us, length us, event | category | flops | bytes accessed | tf_op | source)
XLA Modules:
  0.0 18.5 jit_solution(11131706063501924375)
XLA Ops:
  0.0 0.0 copy-start
  0.0 1.0 %scale.1 = (bf16[128,128]{1,0:T(8,128)(2,1)S(1)}, s32[1,1,384]{2,1,0:T(1,128)S(4)}, s32[1,1,384]{2,1,0:T(1,128)S(4)}, s32[16,128]{1,0:T(8,128)S(1)}) custom-call(f32[128,128]{1,0:T(8,128)} %prior_hbm.1, s32[1,128]{1,0:T(1,128)} %bitcast.2, s32[1,1,384]{2,1,0:T(1,128)} %out_hbm.1, s32[1,1,384]{2,1,0:T(1,128)} %in_hbm.1, s32[16,128]{1,0:T(8,128)} %bitcast.5), custom_call_target="tpu_custom_call" | custom-call | flops 12884901888 | bytes 98304 | tf_op jit(solution)/shard_map/scale/pallas_call | solution.py:257
  1.0 0.0 copy-start.1
  1.1 4.0 %collective-permute-start.1 = (bf16[128,128]{1,0:T(8,128)(2,1)S(1)}, bf16[128,128]{1,0:T(8,128)(2,1)S(1)}, u32[]{:S(2)}, u32[]{:S(2)}) collective-permute-start(bf16[128,128]{1,0:T(8,128)(2,1)S(1)} %get-tuple-element.13.after_ref.refs_0_), channel_id=1, source_target_pairs={{12,0},{8,4},{4,8},{0,12},{13,1},{9,5},{5,9},{1,13},{14,2},{10,6},... | collective-permute-start | bytes 98312 | tf_op jit(solution)/shard_map/ppermute | solution.py:53
  5.0 0.5 %collective-permute-start = (bf16[128,128]{1,0:T(8,128)(2,1)S(1)}, bf16[128,128]{1,0:T(8,128)(2,1)S(1)}, u32[]{:S(2)}, u32[]{:S(2)}) collective-permute-start(bf16[128,128]{1,0:T(8,128)(2,1)S(1)} %get-tuple-element.13.after_ref.refs_0_), channel_id=1, source_target_pairs={{8,0},{12,4},{0,8},{4,12},{9,1},{13,5},{1,9},{5,13},{10,2},{14,6},... | collective-permute-start | bytes 98312 | tf_op jit(solution)/shard_map/ppermute | solution.py:53
  5.5 0.1 collective-permute-start.2
  6.3 0.0 copy-done
  6.3 2.6 %sum_tiles.1 = (bf16[4,128,256]{2,1,0:T(8,128)(2,1)S(1)}, bf16[4,128,256]{2,1,0:T(8,128)(2,1)S(1)}) custom-call(bf16[128,128]{1,0:T(8,128)(2,1)S(1)} %get-tuple-element.13.after_ref.refs_0_, s32[1,1]{1,0:T(1,128)S(6)} %copy.8.count_ref, s32[1,1,384]{2,1,0:T(1,128)S(4)} %get-tuple-element.14.out_ref, s32[1,1,384]{2,1,0:T(1,128)S(4)} %get-tuple-element.15.in_ref, ...), custom_call_target="tpu_custom_call" | custom-call | flops 6291456 | bytes 12582912 | tf_op jit(solution)/shard_map/sum_tiles/pallas_call | solution.py:282
  8.9 0.0 collective-permute-done.1.refs_2_
  8.9 0.0 collective-permute-done.refs_1_
  8.9 0.0 copy-done.1
  8.9 0.2 %first.1.early_ref = f32[2,264,128]{2,1,0:T(8,128)S(1)} custom-call(bf16[128,128]{1,0:T(8,128)(2,1)S(1)} %get-tuple-element.13.after_ref.refs_0_, bf16[128,128]{1,0:T(8,128)(2,1)S(1)} %collective-permute-done.refs_1_, bf16[128,128]{1,0:T(8,128)(2,1)S(1)} %collective-permute-done.1.refs_2_, ...), custom_call_target="tpu_custom_call" | custom-call | flops 50331648 | bytes 524288 | tf_op jit(solution)/shard_map/first/pallas_call | solution.py:330
  9.2 0.3 %collective-permute-done.2.part_ref = bf16[128,128]{1,0:T(8,128)(2,1)S(1)} collective-permute-done((bf16[128,128]{1,0:T(8,128)(2,1)S(1)}, bf16[128,128]{1,0:T(8,128)(2,1)S(1)}, u32[]{:S(2)}, u32[]{:S(2)}) %collective-permute-start.2) | collective-permute-done | bytes 32800 | tf_op jit(solution)/shard_map/ppermute | solution.py:53
  9.4 0.2 nearest.1.after_ref.mine_ref
  9.6 0.1 collective-permute-start.3
  9.7 0.3 %restart.1.restart_ref.refs_2_ = f32[2,128,128]{2,1,0:T(8,128)S(1)} custom-call(f32[2,264,128]{2,1,0:T(8,128)S(1)} %nearest.1.after_ref.mine_ref, s32[16,128]{1,0:T(8,128)S(1)} %get-tuple-element.18.seeds_ref), custom_call_target="tpu_custom_call" | custom-call | flops 1048576 | bytes 131072 | tf_op jit(solution)/shard_map/restart/pallas_call | solution.py:308
  10.0 1.2 %collective-permute-done.3.theirs_ref = f32[2,264,128]{2,1,0:T(8,128)S(1)} collective-permute-done((f32[2,264,128]{2,1,0:T(8,128)S(1)}, f32[2,264,128]{2,1,0:T(8,128)S(1)}, u32[]{:S(2)}, u32[]{:S(2)}) %collective-permute-start.3) | collective-permute-done | bytes 270368 | tf_op jit(solution)/shard_map/ppermute | solution.py:71
  11.3 1.3 %collective-permute-start.4 = (bf16[2,128,128]{2,1,0:T(8,128)(2,1)S(1)}, bf16[2,128,128]{2,1,0:T(8,128)(2,1)S(1)}, u32[]{:S(2)}, u32[]{:S(2)}) collective-permute-start(bf16[2,128,128]{2,1,0:T(8,128)(2,1)S(1)} %get-tuple-element.19.refs_0_.refs_1_), channel_id=1, source_target_pairs={{24,0},{28,4},{16,8},{20,12},{12,16},{8,20},{4,24},{0,28},{25,1},{... | collective-permute-start | bytes 196616 | tf_op jit(solution)/shard_map/ppermute | solution.py:62
  12.6 0.5 %collective-permute-start.5 = (bf16[128,128]{1,0:T(8,128)(2,1)S(1)}, bf16[128,128]{1,0:T(8,128)(2,1)S(1)}, u32[]{:S(2)}, u32[]{:S(2)}) collective-permute-start(bf16[128,128]{1,0:T(8,128)(2,1)S(1)} %get-tuple-element.20.after_ref), channel_id=1, source_target_pairs={{20,0},{16,4},{28,8},{24,12},{4,16},{0,20},{12,24},{8,28},{21,1},{... | collective-permute-start | bytes 98312 | tf_op jit(solution)/shard_map/ppermute | solution.py:67
  13.1 1.9 %collective-permute-done.4.refs_1_.refs_2_ = bf16[2,128,128]{2,1,0:T(8,128)(2,1)S(1)} collective-permute-done((bf16[2,128,128]{2,1,0:T(8,128)(2,1)S(1)}, bf16[2,128,128]{2,1,0:T(8,128)(2,1)S(1)}, u32[]{:S(2)}, u32[]{:S(2)}) %collective-permute-start.4) | collective-permute-done | bytes 65568 | tf_op jit(solution)/shard_map/ppermute | solution.py:62
  15.0 0.2 second.2.early_ref
  15.2 0.8 %collective-permute-done.5.side_ref = bf16[128,128]{1,0:T(8,128)(2,1)S(1)} collective-permute-done((bf16[128,128]{1,0:T(8,128)(2,1)S(1)}, bf16[128,128]{1,0:T(8,128)(2,1)S(1)}, u32[]{:S(2)}, u32[]{:S(2)}) %collective-permute-start.5) | collective-permute-done | bytes 32800 | tf_op jit(solution)/shard_map/ppermute | solution.py:67
  16.1 0.1 side.2.refs_0_
  16.2 0.8 %collective-permute-start.6 = (f32[128,128]{1,0:T(8,128)S(1)}, f32[128,128]{1,0:T(8,128)S(1)}, u32[]{:S(2)}, u32[]{:S(2)}) collective-permute-start(f32[128,128]{1,0:T(8,128)S(1)} %side.2.refs_0_), channel_id=1, source_target_pairs={{0,16},{16,0},{1,17},{17,1},{2,18},{18,2},{3,19},{19,3},{4,20},{20... | collective-permute-start | bytes 196616 | tf_op jit(solution)/shard_map/ppermute | solution.py:71
  17.0 0.2 second.3.early_ref
  17.2 0.2 side.3.refs_0_
  17.3 0.6 %collective-permute-done.6.refs_1_ = f32[128,128]{1,0:T(8,128)S(1)} collective-permute-done((f32[128,128]{1,0:T(8,128)S(1)}, f32[128,128]{1,0:T(8,128)S(1)}, u32[]{:S(2)}, u32[]{:S(2)}) %collective-permute-start.6) | collective-permute-done | bytes 65568 | tf_op jit(solution)/shard_map/ppermute | solution.py:71
  17.9 0.6 %last.1 = f32[128,128]{1,0:T(8,128)} custom-call(f32[128,128]{1,0:T(8,128)S(1)} %side.3.refs_0_, f32[128,128]{1,0:T(8,128)S(1)} %collective-permute-done.6.refs_1_, f32[2,128,128]{2,1,0:T(8,128)S(1)} %restart.1.restart_ref.refs_2_, s32[1,128]{1,0:T(1,128)S(1)} %bitcast.4), custom_call_target="tpu_custom_call" | custom-call | bytes 196608 | tf_op jit(solution)/shard_map/last/pallas_call | solution.py:319
  (2 shorter events, 0.1 us)
Async XLA Ops:
  0.0 6.3 %copy-start = (bf16[1,1,384,128,128]{4,3,2,1,0:T(8,128)(2,1)S(1)}, bf16[1,1,384,128,128]{4,3,2,1,0:T(8,128)(2,1)}, u32[]{:S(2)}) copy-start(bf16[1,1,384,128,128]{4,3,2,1,0:T(8,128)(2,1)} %tiles_ref.1) | copy-start | bytes 37748740
  1.0 7.9 %copy-start.1 = (s32[128]{0:T(128)S(1)}, s32[128]{0:T(128)}, u32[]{:S(2)}) copy-start(s32[128]{0:T(128)} %param.11) | copy-start | bytes 1540
  1.1 7.9 %collective-permute-start.1 = (bf16[128,128]{1,0:T(8,128)(2,1)S(1)}, bf16[128,128]{1,0:T(8,128)(2,1)S(1)}, u32[]{:S(2)}, u32[]{:S(2)}) collective-permute-start(bf16[128,128]{1,0:T(8,128)(2,1)S(1)} %get-tuple-element.13.after_ref.refs_0_), channel_id=1, source_target_pairs={{12,0},{8,4},{4,8},{0,12},{13,1},{9,5},{5,9},{1,13},{14,2},{10,6},... | collective-permute-start | bytes 98312 | tf_op jit(solution)/shard_map/ppermute | solution.py:53
  5.0 3.9 %collective-permute-start = (bf16[128,128]{1,0:T(8,128)(2,1)S(1)}, bf16[128,128]{1,0:T(8,128)(2,1)S(1)}, u32[]{:S(2)}, u32[]{:S(2)}) collective-permute-start(bf16[128,128]{1,0:T(8,128)(2,1)S(1)} %get-tuple-element.13.after_ref.refs_0_), channel_id=1, source_target_pairs={{8,0},{12,4},{0,8},{4,12},{9,1},{13,5},{1,9},{5,13},{10,2},{14,6},... | collective-permute-start | bytes 98312 | tf_op jit(solution)/shard_map/ppermute | solution.py:53
  5.5 3.9 %collective-permute-start.2 = (bf16[128,128]{1,0:T(8,128)(2,1)S(1)}, bf16[128,128]{1,0:T(8,128)(2,1)S(1)}, u32[]{:S(2)}, u32[]{:S(2)}) collective-permute-start(bf16[128,128]{1,0:T(8,128)(2,1)S(1)} %get-tuple-element.13.after_ref.refs_0_), channel_id=1, source_target_pairs={{4,0},{0,4},{12,8},{8,12},{5,1},{1,5},{13,9},{9,13},{6,2},{2,6},{1... | collective-permute-start | bytes 98312 | tf_op jit(solution)/shard_map/ppermute | solution.py:53
  9.6 1.6 %collective-permute-start.3 = (f32[2,264,128]{2,1,0:T(8,128)S(1)}, f32[2,264,128]{2,1,0:T(8,128)S(1)}, u32[]{:S(2)}, u32[]{:S(2)}) collective-permute-start(f32[2,264,128]{2,1,0:T(8,128)S(1)} %nearest.1.after_ref.mine_ref), channel_id=1, source_target_pairs={{0,16},{16,0},{1,17},{17,1},{2,18},{18,2},{3,19},{19,3},{4,20},{20... | collective-permute-start | bytes 811016 | tf_op jit(solution)/shard_map/ppermute | solution.py:71
  11.3 3.7 %collective-permute-start.4 = (bf16[2,128,128]{2,1,0:T(8,128)(2,1)S(1)}, bf16[2,128,128]{2,1,0:T(8,128)(2,1)S(1)}, u32[]{:S(2)}, u32[]{:S(2)}) collective-permute-start(bf16[2,128,128]{2,1,0:T(8,128)(2,1)S(1)} %get-tuple-element.19.refs_0_.refs_1_), channel_id=1, source_target_pairs={{24,0},{28,4},{16,8},{20,12},{12,16},{8,20},{4,24},{0,28},{25,1},{... | collective-permute-start | bytes 196616 | tf_op jit(solution)/shard_map/ppermute | solution.py:62
  12.6 3.5 %collective-permute-start.5 = (bf16[128,128]{1,0:T(8,128)(2,1)S(1)}, bf16[128,128]{1,0:T(8,128)(2,1)S(1)}, u32[]{:S(2)}, u32[]{:S(2)}) collective-permute-start(bf16[128,128]{1,0:T(8,128)(2,1)S(1)} %get-tuple-element.20.after_ref), channel_id=1, source_target_pairs={{20,0},{16,4},{28,8},{24,12},{4,16},{0,20},{12,24},{8,28},{21,1},{... | collective-permute-start | bytes 98312 | tf_op jit(solution)/shard_map/ppermute | solution.py:67
  16.2 1.7 %collective-permute-start.6 = (f32[128,128]{1,0:T(8,128)S(1)}, f32[128,128]{1,0:T(8,128)S(1)}, u32[]{:S(2)}, u32[]{:S(2)}) collective-permute-start(f32[128,128]{1,0:T(8,128)S(1)} %side.2.refs_0_), channel_id=1, source_target_pairs={{0,16},{16,0},{1,17},{17,1},{2,18},{18,2},{3,19},{19,3},{4,20},{20... | collective-permute-start | bytes 196616 | tf_op jit(solution)/shard_map/ppermute | solution.py:71

commit v6 on v4

--- a/solution.py
+++ b/solution.py
@@ -193,9 +193,16 @@
 
 def nearest_kernel(early_ref, part_ref, own_ref, other_ref, given_ref):
     col = lax.axis_index("col")
-    sets = part_ref.shape[0]
-    for place, weight_ref in enumerate((own_ref, other_ref)):
-        given_ref[place, :sets] = early_ref[place, :sets] + times_weight([part_ref[...]], [weight_ref[col ^ 1]])
+    sets, owned = part_ref.shape
+    terms = jnp.dot(
+        part_ref[...],
+        jnp.concatenate([own_ref[col ^ 1], other_ref[col ^ 1]], axis=1),
+        preferred_element_type=jnp.float32,
+    )
+    for place in range(2):
+        at = 2 * place * owned
+        term = terms[:, at:at + owned] + terms[:, at + owned:at + 2 * owned]
+        given_ref[place, :sets] = early_ref[place, :sets] + term
         given_ref[place, sets:] = early_ref[place, sets:]
 
 

time: 19.1 us -> 18.8 us (0.984); the launches traced: 19.3 us -> 18.7 us
  waiting for transfers between devices: 5.17 us -> 7 us
  Pallas kernels: 5.71 us -> 3.89 us
  starting transfers between devices: 7.64 us -> 7.09 us
    ppermute x3, waiting for transfers between devices: 0.3 us -> 2.11 us  [from_column(): lax.ppermute(value, 'col', [(partner(col, offset, cols), col) for col in...]
    pallas_call x1, Pallas kernels: 2.57 us -> 0.76 us  [local(): call(functools.partial(sum_kernel, rows, cols, owned_blocks), [jax.ShapeD...]
    ppermute x1, starting transfers between devices: 2.35 us -> 1.43 us  [from_hop(): return lax.ppermute(value, ('row', 'col'), pairs)]
    ppermute x2, starting transfers between devices: 0.14 us -> 0.66 us  [swap_rows(): return lax.ppermute(value, 'row', [(0, 1), (1, 0)])]
    ppermute x2, waiting for transfers between devices: 2.12 us -> 1.79 us  [swap_rows(): return lax.ppermute(value, 'row', [(0, 1), (1, 0)])]
    ppermute x1, waiting for transfers between devices: 1.57 us -> 1.89 us  [from_hop(): return lax.ppermute(value, ('row', 'col'), pairs)]
  transfers between devices with their start and end apart: 7 -> 7, of which waited for: 5 -> 6; matrix products, arithmetic and copies ran while one was open for 0% -> 0% of each run, Pallas kernels for 19% -> 10%
where the time goes in v6:
time: 18.8 us; the launch traced here: 18.7 us
  starting transfers between devices  7.09 us (38%)
  waiting for transfers between devices  7 us (37%)
  Pallas kernels  3.89 us (21%)
  between operations  0.75 us (4%)
    ppermute x3, starting transfers between devices, from_column(): lax.ppermute(value, 'col', [(partner(col, offset, cols), col) for col in...  4.6 us
    ppermute x3, waiting for transfers between devices, from_column(): lax.ppermute(value, 'col', [(partner(col, offset, cols), col) for col in...  2.11 us
    ppermute x1, waiting for transfers between devices, from_hop(): return lax.ppermute(value, ('row', 'col'), pairs)  1.89 us
    ppermute x2, waiting for transfers between devices, swap_rows(): return lax.ppermute(value, 'row', [(0, 1), (1, 0)])  1.79 us
    ppermute x1, starting transfers between devices, from_hop(): return lax.ppermute(value, ('row', 'col'), pairs)  1.43 us
    ppermute x1, waiting for transfers between devices, from_side(): return lax.ppermute(value, ('row', 'col'), pairs)  1.21 us
    pallas_call x1, Pallas kernels, local(): call(scale_kernel, [jax.ShapeDtypeStruct((sets, owned), low), pltpu.SMEM(...  1.07 us
    pallas_call x1, Pallas kernels, local(): call(functools.partial(sum_kernel, rows, cols, owned_blocks), [jax.ShapeD...  0.76 us
  transfers between devices with their start and end apart: 7, of which 6 were waited for; matrix products, arithmetic and copies ran while one was open for 0% of the time, Pallas kernels for 10%

profile of v6, /device:TPU:0, one launch (start us, length us, event | category | flops | bytes accessed | tf_op | source)
XLA Modules:
  0.0 18.7 jit_solution(2148918944098354506)
XLA Ops:
  0.0 0.0 copy-start
  0.0 1.1 %scale.1 = (bf16[128,128]{1,0:T(8,128)(2,1)S(1)}, s32[1,1,384]{2,1,0:T(1,128)S(4)}, s32[1,1,384]{2,1,0:T(1,128)S(4)}, s32[16,128]{1,0:T(8,128)S(1)}) custom-call(f32[128,128]{1,0:T(8,128)} %prior_hbm.1, s32[1,128]{1,0:T(1,128)} %bitcast.2, s32[1,1,384]{2,1,0:T(1,128)} %out_hbm.1, s32[1,1,384]{2,1,0:T(1,128)} %in_hbm.1, s32[16,128]{1,0:T(8,128)} %bitcast.5), custom_call_target="tpu_custom_call" | custom-call | flops 12884901888 | bytes 98304 | tf_op jit(solution)/shard_map/scale/pallas_call | solution.py:261
  1.1 0.0 copy-start.1
  1.1 4.0 %collective-permute-start.1 = (bf16[128,128]{1,0:T(8,128)(2,1)S(1)}, bf16[128,128]{1,0:T(8,128)(2,1)S(1)}, u32[]{:S(2)}, u32[]{:S(2)}) collective-permute-start(bf16[128,128]{1,0:T(8,128)(2,1)S(1)} %get-tuple-element.13.after_ref.refs_0_), channel_id=1, source_target_pairs={{12,0},{8,4},{4,8},{0,12},{13,1},{9,5},{5,9},{1,13},{14,2},{10,6},... | collective-permute-start | bytes 98312 | tf_op jit(solution)/shard_map/ppermute | solution.py:52
  5.0 0.5 %collective-permute-start = (bf16[128,128]{1,0:T(8,128)(2,1)S(1)}, bf16[128,128]{1,0:T(8,128)(2,1)S(1)}, u32[]{:S(2)}, u32[]{:S(2)}) collective-permute-start(bf16[128,128]{1,0:T(8,128)(2,1)S(1)} %get-tuple-element.13.after_ref.refs_0_), channel_id=1, source_target_pairs={{8,0},{12,4},{0,8},{4,12},{9,1},{13,5},{1,9},{5,13},{10,2},{14,6},... | collective-permute-start | bytes 98312 | tf_op jit(solution)/shard_map/ppermute | solution.py:52
  5.6 0.1 collective-permute-start.2
  6.3 0.0 copy-done
  6.4 0.8 %sum_tiles.1 = (bf16[4,128,256]{2,1,0:T(8,128)(2,1)S(1)}, bf16[4,128,256]{2,1,0:T(8,128)(2,1)S(1)}) custom-call(bf16[128,128]{1,0:T(8,128)(2,1)S(1)} %get-tuple-element.13.after_ref.refs_0_, s32[1,1]{1,0:T(1,128)S(6)} %copy.8.count_ref, s32[1,1,384]{2,1,0:T(1,128)S(4)} %get-tuple-element.14.out_ref, s32[1,1,384]{2,1,0:T(1,128)S(4)} %get-tuple-element.15.in_ref, ...), custom_call_target="tpu_custom_call" | custom-call | flops 6291456 | bytes 12582912 | tf_op jit(solution)/shard_map/sum_tiles/pallas_call | solution.py:286
  7.1 0.0 collective-permute-done.1.refs_2_
  7.1 1.8 %collective-permute-done.refs_1_ = bf16[128,128]{1,0:T(8,128)(2,1)S(1)} collective-permute-done((bf16[128,128]{1,0:T(8,128)(2,1)S(1)}, bf16[128,128]{1,0:T(8,128)(2,1)S(1)}, u32[]{:S(2)}, u32[]{:S(2)}) %collective-permute-start) | collective-permute-done | bytes 32800 | tf_op jit(solution)/shard_map/ppermute | solution.py:52
  9.0 0.0 copy-done.1
  9.0 0.2 %first.1.early_ref = f32[2,264,128]{2,1,0:T(8,128)S(1)} custom-call(bf16[128,128]{1,0:T(8,128)(2,1)S(1)} %get-tuple-element.13.after_ref.refs_0_, bf16[128,128]{1,0:T(8,128)(2,1)S(1)} %collective-permute-done.refs_1_, bf16[128,128]{1,0:T(8,128)(2,1)S(1)} %collective-permute-done.1.refs_2_, ...), custom_call_target="tpu_custom_call" | custom-call | flops 50331648 | bytes 524288 | tf_op jit(solution)/shard_map/first/pallas_call | solution.py:334
  9.2 0.3 %collective-permute-done.2.part_ref = bf16[128,128]{1,0:T(8,128)(2,1)S(1)} collective-permute-done((bf16[128,128]{1,0:T(8,128)(2,1)S(1)}, bf16[128,128]{1,0:T(8,128)(2,1)S(1)}, u32[]{:S(2)}, u32[]{:S(2)}) %collective-permute-start.2) | collective-permute-done | bytes 32800 | tf_op jit(solution)/shard_map/ppermute | solution.py:52
  9.5 0.2 nearest.1.after_ref.mine_ref
  9.7 0.1 collective-permute-start.3
  9.7 0.3 %restart.1.restart_ref.refs_2_ = f32[2,128,128]{2,1,0:T(8,128)S(1)} custom-call(f32[2,264,128]{2,1,0:T(8,128)S(1)} %nearest.1.after_ref.mine_ref, s32[16,128]{1,0:T(8,128)S(1)} %get-tuple-element.18.seeds_ref), custom_call_target="tpu_custom_call" | custom-call | flops 1048576 | bytes 131072 | tf_op jit(solution)/shard_map/restart/pallas_call | solution.py:312
  10.0 1.2 %collective-permute-done.3.theirs_ref = f32[2,264,128]{2,1,0:T(8,128)S(1)} collective-permute-done((f32[2,264,128]{2,1,0:T(8,128)S(1)}, f32[2,264,128]{2,1,0:T(8,128)S(1)}, u32[]{:S(2)}, u32[]{:S(2)}) %collective-permute-start.3) | collective-permute-done | bytes 270368 | tf_op jit(solution)/shard_map/ppermute | solution.py:70
  11.3 1.4 %collective-permute-start.4 = (bf16[2,128,128]{2,1,0:T(8,128)(2,1)S(1)}, bf16[2,128,128]{2,1,0:T(8,128)(2,1)S(1)}, u32[]{:S(2)}, u32[]{:S(2)}) collective-permute-start(bf16[2,128,128]{2,1,0:T(8,128)(2,1)S(1)} %get-tuple-element.19.refs_0_.refs_1_), channel_id=1, source_target_pairs={{24,0},{28,4},{16,8},{20,12},{12,16},{8,20},{4,24},{0,28},{25,1},{... | collective-permute-start | bytes 196616 | tf_op jit(solution)/shard_map/ppermute | solution.py:61
  12.7 0.4 %collective-permute-start.5 = (bf16[128,128]{1,0:T(8,128)(2,1)S(1)}, bf16[128,128]{1,0:T(8,128)(2,1)S(1)}, u32[]{:S(2)}, u32[]{:S(2)}) collective-permute-start(bf16[128,128]{1,0:T(8,128)(2,1)S(1)} %get-tuple-element.20.after_ref), channel_id=1, source_target_pairs={{20,0},{16,4},{28,8},{24,12},{4,16},{0,20},{12,24},{8,28},{21,1},{... | collective-permute-start | bytes 98312 | tf_op jit(solution)/shard_map/ppermute | solution.py:66
  13.2 1.9 %collective-permute-done.4.refs_1_.refs_2_ = bf16[2,128,128]{2,1,0:T(8,128)(2,1)S(1)} collective-permute-done((bf16[2,128,128]{2,1,0:T(8,128)(2,1)S(1)}, bf16[2,128,128]{2,1,0:T(8,128)(2,1)S(1)}, u32[]{:S(2)}, u32[]{:S(2)}) %collective-permute-start.4) | collective-permute-done | bytes 65568 | tf_op jit(solution)/shard_map/ppermute | solution.py:61
  15.1 0.2 second.2.early_ref
  15.2 1.2 %collective-permute-done.5.side_ref = bf16[128,128]{1,0:T(8,128)(2,1)S(1)} collective-permute-done((bf16[128,128]{1,0:T(8,128)(2,1)S(1)}, bf16[128,128]{1,0:T(8,128)(2,1)S(1)}, u32[]{:S(2)}, u32[]{:S(2)}) %collective-permute-start.5) | collective-permute-done | bytes 32800 | tf_op jit(solution)/shard_map/ppermute | solution.py:66
  16.5 0.1 side.2.refs_0_
  16.6 0.6 %collective-permute-start.6 = (f32[128,128]{1,0:T(8,128)S(1)}, f32[128,128]{1,0:T(8,128)S(1)}, u32[]{:S(2)}, u32[]{:S(2)}) collective-permute-start(f32[128,128]{1,0:T(8,128)S(1)} %side.2.refs_0_), channel_id=1, source_target_pairs={{0,16},{16,0},{1,17},{17,1},{2,18},{18,2},{3,19},{19,3},{4,20},{20... | collective-permute-start | bytes 196616 | tf_op jit(solution)/shard_map/ppermute | solution.py:70
  17.2 0.2 second.3.early_ref
  17.4 0.2 side.3.refs_0_
  17.5 0.6 %collective-permute-done.6.refs_1_ = f32[128,128]{1,0:T(8,128)S(1)} collective-permute-done((f32[128,128]{1,0:T(8,128)S(1)}, f32[128,128]{1,0:T(8,128)S(1)}, u32[]{:S(2)}, u32[]{:S(2)}) %collective-permute-start.6) | collective-permute-done | bytes 65568 | tf_op jit(solution)/shard_map/ppermute | solution.py:70
  18.1 0.6 %last.1 = f32[128,128]{1,0:T(8,128)} custom-call(f32[128,128]{1,0:T(8,128)S(1)} %side.3.refs_0_, f32[128,128]{1,0:T(8,128)S(1)} %collective-permute-done.6.refs_1_, f32[2,128,128]{2,1,0:T(8,128)S(1)} %restart.1.restart_ref.refs_2_, s32[1,128]{1,0:T(1,128)S(1)} %bitcast.4), custom_call_target="tpu_custom_call" | custom-call | bytes 196608 | tf_op jit(solution)/shard_map/last/pallas_call | solution.py:323
  (2 shorter events, 0.1 us)
Async XLA Ops:
  0.0 6.3 %copy-start = (bf16[1,1,384,128,128]{4,3,2,1,0:T(8,128)(2,1)S(1)}, bf16[1,1,384,128,128]{4,3,2,1,0:T(8,128)(2,1)}, u32[]{:S(2)}) copy-start(bf16[1,1,384,128,128]{4,3,2,1,0:T(8,128)(2,1)} %tiles_ref.1) | copy-start | bytes 37748740
  1.1 7.9 %copy-start.1 = (s32[128]{0:T(128)S(1)}, s32[128]{0:T(128)}, u32[]{:S(2)}) copy-start(s32[128]{0:T(128)} %param.11) | copy-start | bytes 1540
  1.1 6.0 %collective-permute-start.1 = (bf16[128,128]{1,0:T(8,128)(2,1)S(1)}, bf16[128,128]{1,0:T(8,128)(2,1)S(1)}, u32[]{:S(2)}, u32[]{:S(2)}) collective-permute-start(bf16[128,128]{1,0:T(8,128)(2,1)S(1)} %get-tuple-element.13.after_ref.refs_0_), channel_id=1, source_target_pairs={{12,0},{8,4},{4,8},{0,12},{13,1},{9,5},{5,9},{1,13},{14,2},{10,6},... | collective-permute-start | bytes 98312 | tf_op jit(solution)/shard_map/ppermute | solution.py:52
  5.0 3.9 %collective-permute-start = (bf16[128,128]{1,0:T(8,128)(2,1)S(1)}, bf16[128,128]{1,0:T(8,128)(2,1)S(1)}, u32[]{:S(2)}, u32[]{:S(2)}) collective-permute-start(bf16[128,128]{1,0:T(8,128)(2,1)S(1)} %get-tuple-element.13.after_ref.refs_0_), channel_id=1, source_target_pairs={{8,0},{12,4},{0,8},{4,12},{9,1},{13,5},{1,9},{5,13},{10,2},{14,6},... | collective-permute-start | bytes 98312 | tf_op jit(solution)/shard_map/ppermute | solution.py:52
  5.6 3.9 %collective-permute-start.2 = (bf16[128,128]{1,0:T(8,128)(2,1)S(1)}, bf16[128,128]{1,0:T(8,128)(2,1)S(1)}, u32[]{:S(2)}, u32[]{:S(2)}) collective-permute-start(bf16[128,128]{1,0:T(8,128)(2,1)S(1)} %get-tuple-element.13.after_ref.refs_0_), channel_id=1, source_target_pairs={{4,0},{0,4},{12,8},{8,12},{5,1},{1,5},{13,9},{9,13},{6,2},{2,6},{1... | collective-permute-start | bytes 98312 | tf_op jit(solution)/shard_map/ppermute | solution.py:52
  9.7 1.6 %collective-permute-start.3 = (f32[2,264,128]{2,1,0:T(8,128)S(1)}, f32[2,264,128]{2,1,0:T(8,128)S(1)}, u32[]{:S(2)}, u32[]{:S(2)}) collective-permute-start(f32[2,264,128]{2,1,0:T(8,128)S(1)} %nearest.1.after_ref.mine_ref), channel_id=1, source_target_pairs={{0,16},{16,0},{1,17},{17,1},{2,18},{18,2},{3,19},{19,3},{4,20},{20... | collective-permute-start | bytes 811016 | tf_op jit(solution)/shard_map/ppermute | solution.py:70
  11.3 3.7 %collective-permute-start.4 = (bf16[2,128,128]{2,1,0:T(8,128)(2,1)S(1)}, bf16[2,128,128]{2,1,0:T(8,128)(2,1)S(1)}, u32[]{:S(2)}, u32[]{:S(2)}) collective-permute-start(bf16[2,128,128]{2,1,0:T(8,128)(2,1)S(1)} %get-tuple-element.19.refs_0_.refs_1_), channel_id=1, source_target_pairs={{24,0},{28,4},{16,8},{20,12},{12,16},{8,20},{4,24},{0,28},{25,1},{... | collective-permute-start | bytes 196616 | tf_op jit(solution)/shard_map/ppermute | solution.py:61
  12.7 3.7 %collective-permute-start.5 = (bf16[128,128]{1,0:T(8,128)(2,1)S(1)}, bf16[128,128]{1,0:T(8,128)(2,1)S(1)}, u32[]{:S(2)}, u32[]{:S(2)}) collective-permute-start(bf16[128,128]{1,0:T(8,128)(2,1)S(1)} %get-tuple-element.20.after_ref), channel_id=1, source_target_pairs={{20,0},{16,4},{28,8},{24,12},{4,16},{0,20},{12,24},{8,28},{21,1},{... | collective-permute-start | bytes 98312 | tf_op jit(solution)/shard_map/ppermute | solution.py:66
  16.6 1.5 %collective-permute-start.6 = (f32[128,128]{1,0:T(8,128)S(1)}, f32[128,128]{1,0:T(8,128)S(1)}, u32[]{:S(2)}, u32[]{:S(2)}) collective-permute-start(f32[128,128]{1,0:T(8,128)S(1)} %side.2.refs_0_), channel_id=1, source_target_pairs={{0,16},{16,0},{1,17},{17,1},{2,18},{18,2},{3,19},{19,3},{4,20},{20... | collective-permute-start | bytes 196616 | tf_op jit(solution)/shard_map/ppermute | solution.py:70

commit v7 on v4

--- a/solution.py
+++ b/solution.py
@@ -21,7 +21,7 @@
 TILES_VMEM = 32 * 1024 * 1024
 SMALL_VMEM = 8 * 1024 * 1024
 STRIPS = 4
-UNROLL = 32
+UNROLL = 64
 DEGREE_LINES = 8
 
 

time: 19.1 us -> 19 us (level)
  Pallas kernels: 5.71 us -> 4.1 us
  waiting for transfers between devices: 5.17 us -> 6.62 us
    ppermute x3, waiting for transfers between devices: 0.3 us -> 1.91 us  [from_column(): lax.ppermute(value, 'col', [(partner(col, offset, cols), col) for col in...]
    pallas_call x1, Pallas kernels: 2.57 us -> 0.96 us  [local(): call(functools.partial(sum_kernel, rows, cols, owned_blocks), [jax.ShapeD...]
  transfers between devices with their start and end apart: 7 -> 7, of which waited for: 5 -> 6; matrix products, arithmetic and copies ran while one was open for 0% -> 0% of each run, Pallas kernels for 19% -> 11%
where the time goes in v7:
time: 19 us; the launch traced here: 19.1 us
  starting transfers between devices  7.66 us (40%)
  waiting for transfers between devices  6.62 us (35%)
  Pallas kernels  4.1 us (22%)
  between operations  0.76 us (4%)
    ppermute x3, starting transfers between devices, from_column(): lax.ppermute(value, 'col', [(partner(col, offset, cols), col) for col in...  4.6 us
    ppermute x1, starting transfers between devices, from_hop(): return lax.ppermute(value, ('row', 'col'), pairs)  2.37 us
    ppermute x2, waiting for transfers between devices, swap_rows(): return lax.ppermute(value, 'row', [(0, 1), (1, 0)])  2.12 us
    ppermute x3, waiting for transfers between devices, from_column(): lax.ppermute(value, 'col', [(partner(col, offset, cols), col) for col in...  1.91 us
    ppermute x1, waiting for transfers between devices, from_hop(): return lax.ppermute(value, ('row', 'col'), pairs)  1.39 us
    ppermute x1, waiting for transfers between devices, from_side(): return lax.ppermute(value, ('row', 'col'), pairs)  1.19 us
    pallas_call x1, Pallas kernels, local(): call(scale_kernel, [jax.ShapeDtypeStruct((sets, owned), low), pltpu.SMEM(...  1.07 us
    pallas_call x1, Pallas kernels, local(): call(functools.partial(sum_kernel, rows, cols, owned_blocks), [jax.ShapeD...  0.96 us
  transfers between devices with their start and end apart: 7, of which 6 were waited for; matrix products, arithmetic and copies ran while one was open for 0% of the time, Pallas kernels for 11%

profile of v7, /device:TPU:0, one launch (start us, length us, event | category | flops | bytes accessed | tf_op | source)
XLA Modules:
  0.0 19.1 jit_solution(13505980847780801126)
XLA Ops:
  0.0 0.0 copy-start
  0.0 1.1 %scale.1 = (bf16[128,128]{1,0:T(8,128)(2,1)S(1)}, s32[1,1,384]{2,1,0:T(1,128)S(4)}, s32[1,1,384]{2,1,0:T(1,128)S(4)}, s32[16,128]{1,0:T(8,128)S(1)}) custom-call(f32[128,128]{1,0:T(8,128)} %prior_hbm.1, s32[1,128]{1,0:T(1,128)} %bitcast.2, s32[1,1,384]{2,1,0:T(1,128)} %out_hbm.1, s32[1,1,384]{2,1,0:T(1,128)} %in_hbm.1, s32[16,128]{1,0:T(8,128)} %bitcast.5), custom_call_target="tpu_custom_call" | custom-call | flops 12884901888 | bytes 98304 | tf_op jit(solution)/shard_map/scale/pallas_call | solution.py:254
  1.1 0.0 copy-start.1
  1.1 4.0 %collective-permute-start.1 = (bf16[128,128]{1,0:T(8,128)(2,1)S(1)}, bf16[128,128]{1,0:T(8,128)(2,1)S(1)}, u32[]{:S(2)}, u32[]{:S(2)}) collective-permute-start(bf16[128,128]{1,0:T(8,128)(2,1)S(1)} %get-tuple-element.13.after_ref.refs_0_), channel_id=1, source_target_pairs={{12,0},{8,4},{4,8},{0,12},{13,1},{9,5},{5,9},{1,13},{14,2},{10,6},... | collective-permute-start | bytes 98312 | tf_op jit(solution)/shard_map/ppermute | solution.py:52
  5.0 0.5 %collective-permute-start = (bf16[128,128]{1,0:T(8,128)(2,1)S(1)}, bf16[128,128]{1,0:T(8,128)(2,1)S(1)}, u32[]{:S(2)}, u32[]{:S(2)}) collective-permute-start(bf16[128,128]{1,0:T(8,128)(2,1)S(1)} %get-tuple-element.13.after_ref.refs_0_), channel_id=1, source_target_pairs={{8,0},{12,4},{0,8},{4,12},{9,1},{13,5},{1,9},{5,13},{10,2},{14,6},... | collective-permute-start | bytes 98312 | tf_op jit(solution)/shard_map/ppermute | solution.py:52
  5.6 0.1 collective-permute-start.2
  6.3 0.0 copy-done
  6.4 1.0 %sum_tiles.1 = (bf16[4,128,256]{2,1,0:T(8,128)(2,1)S(1)}, bf16[4,128,256]{2,1,0:T(8,128)(2,1)S(1)}) custom-call(bf16[128,128]{1,0:T(8,128)(2,1)S(1)} %get-tuple-element.13.after_ref.refs_0_, s32[1,1]{1,0:T(1,128)S(6)} %copy.8.count_ref, s32[1,1,384]{2,1,0:T(1,128)S(4)} %get-tuple-element.14.out_ref, s32[1,1,384]{2,1,0:T(1,128)S(4)} %get-tuple-element.15.in_ref, ...), custom_call_target="tpu_custom_call" | custom-call | flops 6291456 | bytes 12582912 | tf_op jit(solution)/shard_map/sum_tiles/pallas_call | solution.py:279
  7.3 0.0 collective-permute-done.1.refs_2_
  7.3 1.6 %collective-permute-done.refs_1_ = bf16[128,128]{1,0:T(8,128)(2,1)S(1)} collective-permute-done((bf16[128,128]{1,0:T(8,128)(2,1)S(1)}, bf16[128,128]{1,0:T(8,128)(2,1)S(1)}, u32[]{:S(2)}, u32[]{:S(2)}) %collective-permute-start) | collective-permute-done | bytes 32800 | tf_op jit(solution)/shard_map/ppermute | solution.py:52
  9.0 0.0 copy-done.1
  9.0 0.2 %first.1.early_ref = f32[2,264,128]{2,1,0:T(8,128)S(1)} custom-call(bf16[128,128]{1,0:T(8,128)(2,1)S(1)} %get-tuple-element.13.after_ref.refs_0_, bf16[128,128]{1,0:T(8,128)(2,1)S(1)} %collective-permute-done.refs_1_, bf16[128,128]{1,0:T(8,128)(2,1)S(1)} %collective-permute-done.1.refs_2_, ...), custom_call_target="tpu_custom_call" | custom-call | flops 50331648 | bytes 524288 | tf_op jit(solution)/shard_map/first/pallas_call | solution.py:327
  9.2 0.3 %collective-permute-done.2.part_ref = bf16[128,128]{1,0:T(8,128)(2,1)S(1)} collective-permute-done((bf16[128,128]{1,0:T(8,128)(2,1)S(1)}, bf16[128,128]{1,0:T(8,128)(2,1)S(1)}, u32[]{:S(2)}, u32[]{:S(2)}) %collective-permute-start.2) | collective-permute-done | bytes 32800 | tf_op jit(solution)/shard_map/ppermute | solution.py:52
  9.5 0.2 nearest.1.after_ref.mine_ref
  9.7 0.1 collective-permute-start.3
  9.7 0.3 %restart.1.restart_ref.refs_2_ = f32[2,128,128]{2,1,0:T(8,128)S(1)} custom-call(f32[2,264,128]{2,1,0:T(8,128)S(1)} %nearest.1.after_ref.mine_ref, s32[16,128]{1,0:T(8,128)S(1)} %get-tuple-element.18.seeds_ref), custom_call_target="tpu_custom_call" | custom-call | flops 1048576 | bytes 131072 | tf_op jit(solution)/shard_map/restart/pallas_call | solution.py:305
  10.0 1.2 %collective-permute-done.3.theirs_ref = f32[2,264,128]{2,1,0:T(8,128)S(1)} collective-permute-done((f32[2,264,128]{2,1,0:T(8,128)S(1)}, f32[2,264,128]{2,1,0:T(8,128)S(1)}, u32[]{:S(2)}, u32[]{:S(2)}) %collective-permute-start.3) | collective-permute-done | bytes 270368 | tf_op jit(solution)/shard_map/ppermute | solution.py:70
  11.3 2.4 %collective-permute-start.4 = (bf16[2,128,128]{2,1,0:T(8,128)(2,1)S(1)}, bf16[2,128,128]{2,1,0:T(8,128)(2,1)S(1)}, u32[]{:S(2)}, u32[]{:S(2)}) collective-permute-start(bf16[2,128,128]{2,1,0:T(8,128)(2,1)S(1)} %get-tuple-element.19.refs_0_.refs_1_), channel_id=1, source_target_pairs={{24,0},{28,4},{16,8},{20,12},{12,16},{8,20},{4,24},{0,28},{25,1},{... | collective-permute-start | bytes 196616 | tf_op jit(solution)/shard_map/ppermute | solution.py:61
  13.7 0.5 %collective-permute-start.5 = (bf16[128,128]{1,0:T(8,128)(2,1)S(1)}, bf16[128,128]{1,0:T(8,128)(2,1)S(1)}, u32[]{:S(2)}, u32[]{:S(2)}) collective-permute-start(bf16[128,128]{1,0:T(8,128)(2,1)S(1)} %get-tuple-element.20.after_ref), channel_id=1, source_target_pairs={{20,0},{16,4},{28,8},{24,12},{4,16},{0,20},{12,24},{8,28},{21,1},{... | collective-permute-start | bytes 98312 | tf_op jit(solution)/shard_map/ppermute | solution.py:66
  14.3 1.4 %collective-permute-done.4.refs_1_.refs_2_ = bf16[2,128,128]{2,1,0:T(8,128)(2,1)S(1)} collective-permute-done((bf16[2,128,128]{2,1,0:T(8,128)(2,1)S(1)}, bf16[2,128,128]{2,1,0:T(8,128)(2,1)S(1)}, u32[]{:S(2)}, u32[]{:S(2)}) %collective-permute-start.4) | collective-permute-done | bytes 65568 | tf_op jit(solution)/shard_map/ppermute | solution.py:61
  15.6 0.2 second.2.early_ref
  15.8 1.2 %collective-permute-done.5.side_ref = bf16[128,128]{1,0:T(8,128)(2,1)S(1)} collective-permute-done((bf16[128,128]{1,0:T(8,128)(2,1)S(1)}, bf16[128,128]{1,0:T(8,128)(2,1)S(1)}, u32[]{:S(2)}, u32[]{:S(2)}) %collective-permute-start.5) | collective-permute-done | bytes 32800 | tf_op jit(solution)/shard_map/ppermute | solution.py:66
  17.0 0.1 side.2.refs_0_
  17.2 0.1 collective-permute-start.6
  17.3 0.2 second.3.early_ref
  17.5 0.2 side.3.refs_0_
  17.6 0.9 %collective-permute-done.6.refs_1_ = f32[128,128]{1,0:T(8,128)S(1)} collective-permute-done((f32[128,128]{1,0:T(8,128)S(1)}, f32[128,128]{1,0:T(8,128)S(1)}, u32[]{:S(2)}, u32[]{:S(2)}) %collective-permute-start.6) | collective-permute-done | bytes 65568 | tf_op jit(solution)/shard_map/ppermute | solution.py:70
  18.5 0.6 %last.1 = f32[128,128]{1,0:T(8,128)} custom-call(f32[128,128]{1,0:T(8,128)S(1)} %side.3.refs_0_, f32[128,128]{1,0:T(8,128)S(1)} %collective-permute-done.6.refs_1_, f32[2,128,128]{2,1,0:T(8,128)S(1)} %restart.1.restart_ref.refs_2_, s32[1,128]{1,0:T(1,128)S(1)} %bitcast.4), custom_call_target="tpu_custom_call" | custom-call | bytes 196608 | tf_op jit(solution)/shard_map/last/pallas_call | solution.py:316
  (2 shorter events, 0.1 us)
Async XLA Ops:
  0.0 6.3 %copy-start = (bf16[1,1,384,128,128]{4,3,2,1,0:T(8,128)(2,1)S(1)}, bf16[1,1,384,128,128]{4,3,2,1,0:T(8,128)(2,1)}, u32[]{:S(2)}) copy-start(bf16[1,1,384,128,128]{4,3,2,1,0:T(8,128)(2,1)} %tiles_ref.1) | copy-start | bytes 37748740
  1.1 7.9 %copy-start.1 = (s32[128]{0:T(128)S(1)}, s32[128]{0:T(128)}, u32[]{:S(2)}) copy-start(s32[128]{0:T(128)} %param.11) | copy-start | bytes 1540
  1.1 6.2 %collective-permute-start.1 = (bf16[128,128]{1,0:T(8,128)(2,1)S(1)}, bf16[128,128]{1,0:T(8,128)(2,1)S(1)}, u32[]{:S(2)}, u32[]{:S(2)}) collective-permute-start(bf16[128,128]{1,0:T(8,128)(2,1)S(1)} %get-tuple-element.13.after_ref.refs_0_), channel_id=1, source_target_pairs={{12,0},{8,4},{4,8},{0,12},{13,1},{9,5},{5,9},{1,13},{14,2},{10,6},... | collective-permute-start | bytes 98312 | tf_op jit(solution)/shard_map/ppermute | solution.py:52
  5.0 3.9 %collective-permute-start = (bf16[128,128]{1,0:T(8,128)(2,1)S(1)}, bf16[128,128]{1,0:T(8,128)(2,1)S(1)}, u32[]{:S(2)}, u32[]{:S(2)}) collective-permute-start(bf16[128,128]{1,0:T(8,128)(2,1)S(1)} %get-tuple-element.13.after_ref.refs_0_), channel_id=1, source_target_pairs={{8,0},{12,4},{0,8},{4,12},{9,1},{13,5},{1,9},{5,13},{10,2},{14,6},... | collective-permute-start | bytes 98312 | tf_op jit(solution)/shard_map/ppermute | solution.py:52
  5.6 3.9 %collective-permute-start.2 = (bf16[128,128]{1,0:T(8,128)(2,1)S(1)}, bf16[128,128]{1,0:T(8,128)(2,1)S(1)}, u32[]{:S(2)}, u32[]{:S(2)}) collective-permute-start(bf16[128,128]{1,0:T(8,128)(2,1)S(1)} %get-tuple-element.13.after_ref.refs_0_), channel_id=1, source_target_pairs={{4,0},{0,4},{12,8},{8,12},{5,1},{1,5},{13,9},{9,13},{6,2},{2,6},{1... | collective-permute-start | bytes 98312 | tf_op jit(solution)/shard_map/ppermute | solution.py:52
  9.7 1.6 %collective-permute-start.3 = (f32[2,264,128]{2,1,0:T(8,128)S(1)}, f32[2,264,128]{2,1,0:T(8,128)S(1)}, u32[]{:S(2)}, u32[]{:S(2)}) collective-permute-start(f32[2,264,128]{2,1,0:T(8,128)S(1)} %nearest.1.after_ref.mine_ref), channel_id=1, source_target_pairs={{0,16},{16,0},{1,17},{17,1},{2,18},{18,2},{3,19},{19,3},{4,20},{20... | collective-permute-start | bytes 811016 | tf_op jit(solution)/shard_map/ppermute | solution.py:70
  11.3 4.3 %collective-permute-start.4 = (bf16[2,128,128]{2,1,0:T(8,128)(2,1)S(1)}, bf16[2,128,128]{2,1,0:T(8,128)(2,1)S(1)}, u32[]{:S(2)}, u32[]{:S(2)}) collective-permute-start(bf16[2,128,128]{2,1,0:T(8,128)(2,1)S(1)} %get-tuple-element.19.refs_0_.refs_1_), channel_id=1, source_target_pairs={{24,0},{28,4},{16,8},{20,12},{12,16},{8,20},{4,24},{0,28},{25,1},{... | collective-permute-start | bytes 196616 | tf_op jit(solution)/shard_map/ppermute | solution.py:61
  13.7 3.3 %collective-permute-start.5 = (bf16[128,128]{1,0:T(8,128)(2,1)S(1)}, bf16[128,128]{1,0:T(8,128)(2,1)S(1)}, u32[]{:S(2)}, u32[]{:S(2)}) collective-permute-start(bf16[128,128]{1,0:T(8,128)(2,1)S(1)} %get-tuple-element.20.after_ref), channel_id=1, source_target_pairs={{20,0},{16,4},{28,8},{24,12},{4,16},{0,20},{12,24},{8,28},{21,1},{... | collective-permute-start | bytes 98312 | tf_op jit(solution)/shard_map/ppermute | solution.py:66
  17.2 1.3 %collective-permute-start.6 = (f32[128,128]{1,0:T(8,128)S(1)}, f32[128,128]{1,0:T(8,128)S(1)}, u32[]{:S(2)}, u32[]{:S(2)}) collective-permute-start(f32[128,128]{1,0:T(8,128)S(1)} %side.2.refs_0_), channel_id=1, source_target_pairs={{0,16},{16,0},{1,17},{17,1},{2,18},{18,2},{3,19},{19,3},{4,20},{20... | collective-permute-start | bytes 196616 | tf_op jit(solution)/shard_map/ppermute | solution.py:70
